TPU v7x, 128 devices: a whole 4x4x4 slice. The times are simulated.
128 devices in a mesh: row: 16 (over y, x), col: 8 (over z, core).
Axes of the slice: x: 4, y: 4, z: 4, core: 2. Of those that a mesh axis runs over, the one named last changes fastest.
Arguments:
- child_blocks: float32 [16384, 8192], P('row', 'col'), as said below
- block_map: int32 [2, 64], replicated, may hold values from 0 to 127, as said below
- front_diagonal: float32 [16384], replicated, may hold values from 40 to 80
Outputs:
- front: float32 [16384, 16384], P('row', 'col')
Inputs may be any that keep to these rules, and one draw needn't show every extreme that they name: `child_blocks`: each child's block is symmetric: X_c transposed equals X_c. Each panel's pivot block front[K, K], as it stands before panel k, is symmetric positive definite. For each child the 64 entries of block_map[c] are distinct. Split them into 8 aligned groups of 8 in order: each group names exactly 1 block in every range of 16 consecutive parent blocks starting at a multiple of 16, and at most 1 in every such range of 8; for each child some range of 8 gets exactly 1 from every group.
All inputs are finite; a program needn't handle non-finite values.
Results may differ from a plain program's by a relative error of at most 0.0001.
Values sent between devices are 32-bit elements; how exact they have to be, the bound alone decides.
A program may use at most 128 MiB of HBM per device.

v0:
```python
import jax
import jax.numpy as jnp
from jax import lax
from jax.sharding import PartitionSpec as P

F = 16384
BLK = 128
PW = 512


def spread(value, axis, source):
    kept = jnp.where(lax.axis_index(axis) == source, value, 0).astype(value.dtype)
    return lax.psum(kept, axis)


def rank_within(targets, range_count):
    matches = (targets[..., None] == jnp.arange(range_count, dtype=jnp.int32)).astype(jnp.int32)
    earlier = jnp.cumsum(matches, axis=-2) - matches
    return jnp.sum(earlier * matches, axis=-1)


def send_table(targets, range_count, capacity):
    rank_ids = rank_within(targets, range_count)
    places = jnp.arange(targets.shape[0], dtype=jnp.int32)
    wanted = (targets[:, None, None] == jnp.arange(range_count, dtype=jnp.int32)[None, :, None]) & (
        rank_ids[:, None, None] == jnp.arange(capacity, dtype=jnp.int32)[None, None, :]
    )
    return (jnp.sum(jnp.where(wanted, places[:, None, None] + 1, 0), axis=0) - 1).reshape(-1)


def receive_table(
    child_map, group_count, range_count, range_size, capacity, range_here, source_first
):
    grouped = child_map.reshape(group_count, -1)
    rank_ids = rank_within(grouped // range_size, range_count)
    sources = source_first + jnp.arange(group_count, dtype=jnp.int32)[:, None]
    slot_ids = (sources * capacity + rank_ids).reshape(-1)
    wanted = (
        child_map[None, :]
        == (range_here * range_size + jnp.arange(range_size, dtype=jnp.int32))[:, None]
    )
    return jnp.sum(jnp.where(wanted, slot_ids[None, :] + 1, 0), axis=1) - 1


def take_masked(blocks, slot_table, which_axis):
    gathered = jnp.take(blocks, jnp.maximum(slot_table, 0), axis=which_axis)
    mask_shape = [1] * gathered.ndim
    mask_shape[which_axis] = slot_table.shape[0]
    return gathered * (slot_table >= 0).astype(gathered.dtype).reshape(mask_shape)


def invert(pivot_block):
    normal_matrix = jnp.dot(
        pivot_block.T,
        pivot_block,
        precision=lax.Precision.HIGHEST,
        preferred_element_type=jnp.float32,
    )
    lower_chol = jnp.linalg.cholesky(normal_matrix)
    return jax.scipy.linalg.cho_solve((lower_chol, True), pivot_block.T)


def body(child_blocks, block_map, front_diagonal):
    row_devices = lax.axis_size("row")
    col_devices = lax.axis_size("col")
    half_rows = row_devices // 2
    row_here = lax.axis_index("row")
    col_here = lax.axis_index("col")
    child_here = row_here // half_rows
    group_here = row_here % half_rows
    group_size = child_blocks.shape[1] // BLK
    col_capacity = group_size // col_devices
    row_capacity = (col_capacity + 1) // 2
    row_range = F // (BLK * row_devices)
    col_range = F // (BLK * col_devices)
    tile_rows = row_range * BLK
    tile_cols = col_range * BLK
    col_slots_all = col_devices * col_capacity
    my_map = jnp.take(block_map, child_here, axis=0)
    my_rows = lax.dynamic_slice_in_dim(my_map, group_here * group_size, group_size)
    row_table = send_table(my_rows // row_range, row_devices, row_capacity)

    def col_send(child_map):
        my_cols = lax.dynamic_slice_in_dim(child_map, col_here * group_size, group_size)
        return send_table(my_cols // col_range, col_devices, col_capacity)

    pieces = child_blocks.reshape(group_size, BLK, child_blocks.shape[1])
    outgoing = take_masked(pieces, row_table, 0)
    arrived = lax.all_to_all(outgoing, "row", split_axis=0, concat_axis=0, tiled=True)
    both_tables = jnp.stack([col_send(block_map[0]), col_send(block_map[1])])
    source_tables = jnp.take(
        both_tables, jnp.arange(row_devices, dtype=jnp.int32) // half_rows, axis=0
    )
    quarters = arrived.reshape(row_devices, row_capacity * BLK, group_size, BLK)
    selected = jax.vmap(
        lambda source_block, source_table: take_masked(source_block, source_table, 1)
    )(quarters, source_tables)
    outgoing = selected.reshape(row_devices * row_capacity * BLK, col_devices, col_capacity * BLK)
    landed = lax.all_to_all(outgoing, "col", split_axis=1, concat_axis=1, tiled=True)
    landed = landed.reshape(row_devices * row_capacity, BLK, col_slots_all, BLK)
    assembled = jnp.zeros((tile_rows, tile_cols), jnp.float32)
    for child_index in range(2):
        child_map = block_map[child_index]
        row_slots = receive_table(
            child_map,
            half_rows,
            row_devices,
            row_range,
            row_capacity,
            row_here,
            child_index * half_rows,
        )
        col_slots = receive_table(
            child_map, col_devices, col_devices, col_range, col_capacity, col_here, 0
        )
        picked = take_masked(landed, row_slots, 0)
        picked = take_masked(picked, col_slots, 2)
        assembled = assembled + picked.reshape(tile_rows, tile_cols)
    global_rows = row_here * tile_rows + jnp.arange(tile_rows, dtype=jnp.int32)
    global_cols = col_here * tile_cols + jnp.arange(tile_cols, dtype=jnp.int32)
    diagonal_here = lax.dynamic_slice_in_dim(front_diagonal, row_here * tile_rows, tile_rows)
    front_tile = assembled + jnp.where(
        global_rows[:, None] == global_cols[None, :], diagonal_here[:, None], 0.0
    )
    first_column = col_here == 0
    for panel_index in range(2):
        start_col = panel_index * PW
        end_col = start_col + PW
        upper_block = spread(front_tile[start_col:end_col, :], "row", 0)
        below_mask = global_rows >= end_col
        inverse = invert(upper_block[:, start_col:end_col])
        factor = jnp.dot(
            front_tile[:, start_col:end_col],
            inverse,
            precision=lax.Precision.HIGHEST,
            preferred_element_type=jnp.float32,
        )
        factor = jnp.where(below_mask[:, None], factor, 0.0)
        factor = spread(factor, "col", 0)
        right_mask = global_cols >= end_col
        upper_part = jnp.where(right_mask[None, :], upper_block, 0.0)
        front_tile = front_tile - jnp.dot(
            factor, upper_part, precision=lax.Precision.HIGHEST, preferred_element_type=jnp.float32
        )
        keep_factor = below_mask[:, None] & first_column
        front_tile = front_tile.at[:, start_col:end_col].set(
            jnp.where(keep_factor, factor, front_tile[:, start_col:end_col])
        )
    return front_tile


def solution(mesh):
    return jax.shard_map(
        body,
        mesh=mesh,
        in_specs=(P("row", "col"), P(), P()),
        out_specs=P("row", "col"),
        check_vma=False,
    )
```

profile of v0, /device:TPU:33, one launch (start us, length us, event | category | flops | bytes accessed | tf_op | source)
XLA Modules:
  0.0 1077.4 jit_solution(5219675450705000822)
XLA Ops:
  7.9 6.7 gather_fusion.1
  14.6 8.9 select_multiply_fusion
  23.5 7.3 all-to-all-start
  33.8 120.2 %all-to-all-done = f32[16,128,1024]{2,1,0:T(8,128)} async-done(((f32[16,128,1024]{2,1,0:T(8,128)}), f32[16,128,1024]{2,1,0:T(8,128)}, u32[]{:S(2)}, u32[]{:S(2)}) %all-to-all-start) | async-done | bytes 8388640 | tf_op jit(solution)/shard_map/all_to_all | solution.py:89
  154.0 9.2 copy.60
  163.2 9.3 copy.63
  172.5 7.9 gather_fusion.2
  180.4 9.9 copy.64
  190.5 5.6 fusion
  196.1 4.9 copy.65
  201.0 6.9 all-to-all-start.1
  209.4 90.8 %all-to-all-done.1 = f32[2048,8,128]{2,0,1:T(8,128)} async-done(((f32[2048,8,128]{2,0,1:T(8,128)}), f32[2048,8,128]{2,0,1:T(8,128)}, u32[]{:S(2)}, u32[]{:S(2)}) %all-to-all-start.1) | async-done | bytes 8388640 | tf_op jit(solution)/shard_map/all_to_all | solution.py:99
  300.2 10.7 copy.66
  310.9 6.1 gather_fusion.3
  317.0 2.5 select_multiply_fusion.2
  319.5 2.7 copy.67
  322.3 6.1 gather_fusion.5
  328.4 2.5 select_multiply_fusion.1
  330.9 2.7 copy.68
  333.6 6.5 gather_fusion.4
  340.1 6.7 gather_fusion.6
  346.8 9.4 fusion.1
  356.2 9.3 copy.69
  365.4 5.5 bitcast_add_fusion
  371.0 3.4 copy-done.1
  374.4 2.7 slice_select_fusion.1
  377.4 102.7 %all-reduce.6.cloned.1.call-done = f32[512,2048]{0,1:T(8,128)} async-done(((f32[512,2048]{0,1:T(8,128)}), f32[512,2048]{0,1:T(8,128)}) %all-reduce.6.cloned.1.call-update) | async-done | bytes 4194320 | tf_op jit(solution)/shard_map/psum | solution.py:13
  480.1 3.4 fusion.44
  484.1 11.7 %cholesky.286 = f32[128,128]{1,0:T(8,128)S(1)} custom-call(f32[128,128]{1,0:T(8,128)S(1)} %cholesky.426), custom_call_target="Cholesky" | custom-call | tf_op jit(solution)/shard_map/jit(cholesky)/cholesky | solution.py:59
  495.9 9.8 custom-call.31
  506.4 12.2 %cholesky.305 = f32[128,128]{1,0:T(8,128)S(1)} custom-call(f32[128,128]{1,0:T(8,128)S(1)} %cholesky.430), custom_call_target="Cholesky" | custom-call | tf_op jit(solution)/shard_map/jit(cholesky)/cholesky | solution.py:59
  519.9 9.8 custom-call.32
  530.4 11.7 %cholesky.326 = f32[128,128]{1,0:T(8,128)S(1)} custom-call(f32[128,128]{1,0:T(8,128)S(1)} %cholesky.435), custom_call_target="Cholesky" | custom-call | tf_op jit(solution)/shard_map/jit(cholesky)/cholesky | solution.py:59
  542.9 9.8 custom-call.33
  553.3 11.9 %cholesky.343 = f32[128,128]{1,0:T(8,128)S(1)} custom-call(f32[128,128]{1,0:T(8,128)S(1)} %convolution_subtract_fusion.17), custom_call_target="Cholesky" | custom-call | tf_op jit(solution)/shard_map/jit(cholesky)/cholesky | solution.py:59
  568.5 7.8 while.7
  569.1 1.3 bitcast_dynamic-update-slice_fusion.4
  575.0 1.3 bitcast_dynamic-update-slice_fusion.4
  576.3 39.3 %custom-call.34 = f32[4,128,128]{1,2,0:T(8,128)S(1)} custom-call(f32[4,128,128]{2,1,0:T(8,128)S(1)} %get-tuple-element.58), custom_call_target="InvertDiagBlocksLowerTriangular" | custom-call | tf_op jit(solution)/shard_map/jit(_cho_solve)/triangular_solve | solution.py:60
  623.2 6.5 select_select_fusion.3
  630.6 60.9 %all-reduce.8.cloned.1.call-done = f32[1024,512]{0,1:T(8,128)} async-done(((f32[1024,512]{0,1:T(8,128)}), f32[1024,512]{0,1:T(8,128)}) %all-reduce.8.cloned.1.call-update) | async-done | bytes 2097168 | tf_op jit(solution)/shard_map/psum | solution.py:13
  691.6 20.0 %fusion.6 = f32[1024,2048]{0,1:T(8,128)S(1)} fusion(f32[1024,2048]{0,1:T(8,128)} %copy-done.1, f32[1024,512]{0,1:T(8,128)} %all-reduce.8.cloned.1.call-done, f32[512,2048]{0,1:T(8,128)} %all-reduce.6.cloned.1.call-done, pred[2048]{0:T(1024)(128)(4,1)S(1)} %fusion.135), kind=kOutput, calls=%fused_computation.26 | convolution fusion | flops 12888047616 | bytes 23070720 | tf_op jit(solution)/shard_map/dot_general | solution.py:142
  712.9 3.4 copy-done
  716.3 2.4 slice_select_fusion
  719.2 106.5 %all-reduce.10.cloned.1.call-done = f32[512,2048]{0,1:T(8,128)} async-done(((f32[512,2048]{0,1:T(8,128)}), f32[512,2048]{0,1:T(8,128)}) %all-reduce.10.cloned.1.call-update) | async-done | bytes 4194320 | tf_op jit(solution)/shard_map/psum | solution.py:13
  825.7 3.4 fusion.42
  829.7 11.7 %cholesky.358 = f32[128,128]{1,0:T(8,128)S(1)} custom-call(f32[128,128]{1,0:T(8,128)S(1)} %cholesky.439), custom_call_target="Cholesky" | custom-call | tf_op jit(solution)/shard_map/jit(cholesky)/cholesky | solution.py:59
  841.6 9.8 custom-call.35
  852.1 11.9 %cholesky.377 = f32[128,128]{1,0:T(8,128)S(1)} custom-call(f32[128,128]{1,0:T(8,128)S(1)} %cholesky.443), custom_call_target="Cholesky" | custom-call | tf_op jit(solution)/shard_map/jit(cholesky)/cholesky | solution.py:59
  865.3 9.8 custom-call.36
  875.8 11.7 %cholesky.398 = f32[128,128]{1,0:T(8,128)S(1)} custom-call(f32[128,128]{1,0:T(8,128)S(1)} %cholesky.448), custom_call_target="Cholesky" | custom-call | tf_op jit(solution)/shard_map/jit(cholesky)/cholesky | solution.py:59
  888.3 9.8 custom-call.37
  898.7 11.9 %cholesky.415 = f32[128,128]{1,0:T(8,128)S(1)} custom-call(f32[128,128]{1,0:T(8,128)S(1)} %convolution_subtract_fusion.16), custom_call_target="Cholesky" | custom-call | tf_op jit(solution)/shard_map/jit(cholesky)/cholesky | solution.py:59
  914.1 8.2 while.8
  914.8 1.4 bitcast_dynamic-update-slice_fusion.5
  916.8 1.4 bitcast_dynamic-update-slice_fusion.5
  918.9 1.4 bitcast_dynamic-update-slice_fusion.5
  920.9 1.4 bitcast_dynamic-update-slice_fusion.5
  922.3 39.3 %custom-call.38 = f32[4,128,128]{1,2,0:T(8,128)S(1)} custom-call(f32[4,128,128]{2,1,0:T(8,128)S(1)} %get-tuple-element.59), custom_call_target="InvertDiagBlocksLowerTriangular" | custom-call | tf_op jit(solution)/shard_map/jit(_cho_solve)/triangular_solve | solution.py:60
  969.1 6.5 select_select_fusion.2
  976.4 61.1 %all-reduce.12.cloned.1.call-done = f32[1024,512]{0,1:T(8,128)} async-done(((f32[1024,512]{0,1:T(8,128)}), f32[1024,512]{0,1:T(8,128)}) %all-reduce.12.cloned.1.call-update) | async-done | bytes 2097168 | tf_op jit(solution)/shard_map/psum | solution.py:13
  1037.5 20.0 %fusion.9 = f32[1024,2048]{0,1:T(8,128)} fusion(f32[1024,2048]{0,1:T(8,128)} %copy-done, f32[1024,512]{0,1:T(8,128)} %all-reduce.12.cloned.1.call-done, f32[512,2048]{0,1:T(8,128)} %all-reduce.10.cloned.1.call-done, pred[2048]{0:T(1024)(128)(4,1)S(1)} %fusion.134), kind=kOutput, calls=%fused_computation.27 | convolution fusion | flops 12888047616 | bytes 23070720 | tf_op jit(solution)/shard_map/dot_general | solution.py:142
  1057.5 4.0 fusion.13
  1061.5 9.1 copy.76
  (192 shorter events, 43.3 us)
Async XLA Ops:
  23.5 130.5 %all-to-all-start = ((f32[16,128,1024]{2,1,0:T(8,128)}), f32[16,128,1024]{2,1,0:T(8,128)}, u32[]{:S(2)}, u32[]{:S(2)}) async-start(f32[16,128,1024]{2,1,0:T(8,128)} %select_multiply_fusion), calls=%async_computation | async-start | bytes 16777216 | tf_op jit(solution)/shard_map/all_to_all | solution.py:89
  201.0 99.2 %all-to-all-start.1 = ((f32[2048,8,128]{2,0,1:T(8,128)}), f32[2048,8,128]{2,0,1:T(8,128)}, u32[]{:S(2)}, u32[]{:S(2)}) async-start(f32[2048,8,128]{2,0,1:T(8,128)} %copy.65), calls=%async_computation.1 | async-start | bytes 16777216 | tf_op jit(solution)/shard_map/all_to_all | solution.py:99
  207.8 272.2 %all-reduce.6.cloned.1.call-start = ((), (), s32[]{:S(2)}) async-start(), calls=%async_computation.2 | async-start | bytes 8388608 | tf_op jit(solution)/shard_map/psum | solution.py:13
  356.2 9.3 dynamic-slice-start
  371.0 3.4 copy-start.1
  377.1 314.5 %all-reduce.8.cloned.1.call-start = ((), (), s32[]{:S(2)}) async-start(), calls=%async_computation.3 | async-start | bytes 4194304 | tf_op jit(solution)/shard_map/psum | solution.py:13
  629.7 196.0 %all-reduce.10.cloned.1.call-start = ((), (), s32[]{:S(2)}) async-start(), calls=%async_computation.4 | async-start | bytes 8388608 | tf_op jit(solution)/shard_map/psum | solution.py:13
  691.6 20.0 %copy-start.3 = (f32[1024,512]{0,1:T(8,128)S(1)}, f32[1024,512]{0,1:T(8,128)}, u32[]{:S(2)}) copy-start(f32[1024,512]{0,1:T(8,128)} %all-reduce.8.cloned.1.call-done) | copy-start | bytes 6291460
  712.9 3.4 copy-start
  718.8 318.8 %all-reduce.12.cloned.1.call-start = ((), (), s32[]{:S(2)}) async-start(), calls=%async_computation.5 | async-start | bytes 4194304 | tf_op jit(solution)/shard_map/psum | solution.py:13
  1037.5 20.0 %copy-start.2 = (f32[1024,512]{0,1:T(8,128)S(1)}, f32[1024,512]{0,1:T(8,128)}, u32[]{:S(2)}) copy-start(f32[1024,512]{0,1:T(8,128)} %all-reduce.12.cloned.1.call-done) | copy-start | bytes 6291460
Sparse Core Ops, SparseCore 0:
  377.2 102.8 all-reduce.5
  629.9 61.6 all-reduce.7
  718.9 106.7 all-reduce.9
  975.8 61.6 all-reduce.11
where the time goes:
time: 1090 us; the launch traced here: 1080 us
  waiting for transfers between devices  542 us (50%)
  other arithmetic  289 us (27%)
  local copies, waits for them, and re-layouts  135 us (12%)
  matrix products  75.8 us (7%)
  between operations  19.4 us (2%)
  starting transfers between devices  15.1 us (1%)
    psum x4, waiting for transfers between devices, spread(): return lax.psum(kept, axis)  331 us
    another operation x30, other arithmetic, invert(): lower_chol = jnp.linalg.cholesky(normal_matrix)  159 us
    all_to_all x1, waiting for transfers between devices, body(): lax.all_to_all(outgoing, 'row', split_axis=0, concat_axis=0, tiled=True)  120 us
    all_to_all x1, waiting for transfers between devices, body(): lax.all_to_all(outgoing, 'col', split_axis=1, concat_axis=1, tiled=True)  90.8 us
    another operation x5, other arithmetic, invert(): return jax.scipy.linalg.cho_solve((lower_chol, True), pivot_block.T)  78.9 us
    gather x9, local copies, waits for them, and re-layouts, take_masked(): gathered = jnp.take(blocks, jnp.maximum(slot_table, 0), axis=which_axis)  50 us
    dot_general x2, matrix products, body(): jnp.dot(factor, upper_part, precision=lax.Precision.HIGHEST, preferred_el...  40 us
  transfers between devices with their start and end apart: 6, of which 6 were waited for; matrix products, arithmetic and copies ran while one was open for 1% of the time, Pallas kernels for 0%

commit v1 on v0

v1 whole, which is shorter than its diff:
```python
import jax
import jax.numpy as jnp
from jax import lax
from jax.experimental import pallas as pl
from jax.experimental.pallas import tpu as pltpu
from jax.sharding import PartitionSpec as P

BLK = 128
PW = 512
TR = 1024
TC = 2048
MESH = pl.DeviceIdType.MESH
VMEM_LIMIT = 56 * 1024 * 1024
ANY = pl.BlockSpec(memory_space=pl.ANY)
SMEM = pl.BlockSpec(memory_space=pltpu.SMEM)
VMEM = pl.BlockSpec(memory_space=pltpu.VMEM)


def pack_kernel(map_ref, child_ref, send_ref, table_ref, sem):
    row, col = lax.axis_index("row"), lax.axis_index("col")
    child, group = row // 8, row % 8

    def start(step, carry):
        t, u = step // 8, step % 8
        q = map_ref[child, group * 8 + t] // 16
        c = map_ref[child, col * 8 + u] // 16
        pltpu.make_async_copy(
            child_ref.at[
                pl.ds(pl.multiple_of(t * BLK, BLK), BLK), pl.ds(pl.multiple_of(u * BLK, BLK), BLK)
            ],
            send_ref.at[q * 8 + c],
            sem,
        ).start()
        return carry

    lax.fori_loop(0, 64, start, 0)

    def clear(step, carry):
        table_ref[step // 32, step % 32] = -1
        return carry

    lax.fori_loop(0, 64, clear, 0)

    def look(step, carry):
        k, s = step // 64, step % 64
        b = map_ref[k, s]

        @pl.when(b // 8 == row)
        def _():
            table_ref[k, b % 8] = s // 8

        @pl.when(b // 16 == col)
        def _():
            table_ref[k, 8 + b % 16] = s // 8

        @pl.when(b < 8)
        def _():
            table_ref[k, 24 + b] = s // 8

        return carry

    lax.fori_loop(0, 128, look, 0)
    pltpu.make_async_copy(send_ref, send_ref, sem).wait()


def pack(block_map, child):
    return pl.pallas_call(
        pack_kernel,
        out_shape=(
            jax.ShapeDtypeStruct((64, BLK, BLK), jnp.float32),
            jax.ShapeDtypeStruct((2, 32), jnp.int32),
        ),
        in_specs=[SMEM, ANY],
        out_specs=(ANY, SMEM),
        scratch_shapes=[pltpu.SemaphoreType.DMA],
        name="pack",
    )(block_map, child)


def exchange_kernel(
    send_ref, recv_ref, strip_ref, main_s, main_r, col_s, col_r, own_sem, gat_s, gat_r
):
    row, col = lax.axis_index("row"), lax.axis_index("col")
    me = row * 8 + col
    x, y = row % 4, row // 4

    own_a = pltpu.make_async_copy(send_ref.at[(row // 2) * 8 + col], recv_ref.at[me], own_sem.at[0])
    own_b = pltpu.make_async_copy(send_ref.at[col * 8], strip_ref.at[y, x, col], own_sem.at[1])
    own_a.start()
    own_b.start()

    def send_strip(step, carry):
        to = (col + step) % 8
        pltpu.make_async_remote_copy(
            send_ref.at[to * 8], strip_ref.at[y, x, col], col_s, col_r,
            device_id=(row, to), device_id_type=MESH,
        ).start()
        return carry

    lax.fori_loop(1, 8, send_strip, 0)

    def send_block(step, carry):
        to = (me + step * 45) % 128
        to_row, to_col = to // 8, to % 8
        pltpu.make_async_remote_copy(
            send_ref.at[(to_row // 2) * 8 + to_col], recv_ref.at[me], main_s, main_r,
            device_id=(to_row, to_col), device_id_type=MESH,
        ).start()
        return carry

    xp, xm = y * 4 + (x + 1) % 4, y * 4 + (x + 3) % 4
    yp, ym = ((y + 1) % 4) * 4 + x, ((y + 3) % 4) * 4 + x
    xl, xr = (x + 3) % 4, (x + 1) % 4
    yl, yr = (y + 3) % 4, (y + 1) % 4

    def hop(index, piece, to_row):
        ref = strip_ref.at[piece]
        return pltpu.make_async_remote_copy(
            ref, ref, gat_s.at[index], gat_r.at[index],
            device_id=(to_row, col), device_id_type=MESH,
        )

    def landed(index, piece):
        ref = strip_ref.at[piece]
        pltpu.make_async_remote_copy(
            ref, ref, gat_s.at[index], gat_r.at[index],
            device_id=(row, col), device_id_type=MESH,
        ).wait_recv()

    lo, hi = pl.ds(0, 4), pl.ds(4, 4)
    two = [pl.ds(2 * i, 2) for i in range(4)]
    every = pl.ds(0, 4)

    seven = strip_ref.at[y, x, pl.ds(0, 7)]
    pltpu.make_async_remote_copy(
        seven, seven, col_s, col_r, device_id=(row, col), device_id_type=MESH
    ).wait()
    own_b.wait()

    hops = []

    def go(index, piece, to_row):
        copy = hop(index, piece, to_row)
        copy.start()
        hops.append(copy)

    go(0, (y, x, lo), xp)
    go(1, (y, x, lo), xm)
    go(2, (y, x, hi), yp)
    go(3, (y, x, hi), ym)
    lax.fori_loop(1, 32, send_block, 0)
    landed(0, (y, xl, lo))
    go(4, (y, xl, two[0]), xp)
    landed(1, (y, xr, lo))
    go(5, (y, xr, two[1]), xm)
    landed(2, (yl, x, hi))
    go(6, (yl, x, two[2]), yp)
    landed(3, (yr, x, hi))
    go(7, (yr, x, two[3]), ym)
    lax.fori_loop(32, 64, send_block, 0)
    xo, yo = (x + 2) % 4, (y + 2) % 4
    landed(4, (y, xo, two[0]))
    landed(5, (y, xo, two[1]))
    go(8, (y, every, lo), yp)
    go(9, (y, every, lo), ym)
    landed(6, (yo, x, two[2]))
    landed(7, (yo, x, two[3]))
    go(10, (every, x, hi), xp)
    go(11, (every, x, hi), xm)
    lax.fori_loop(64, 96, send_block, 0)
    first, last = pl.ds(0, 2), pl.ds(2, 2)
    landed(8, (yl, every, lo))
    go(12, (yl, first, lo), yp)
    landed(9, (yr, every, lo))
    go(13, (yr, last, lo), ym)
    landed(10, (every, xl, hi))
    go(14, (first, xl, hi), xp)
    landed(11, (every, xr, hi))
    go(15, (last, xr, hi), xm)
    lax.fori_loop(96, 128, send_block, 0)
    landed(12, (yo, first, lo))
    landed(13, (yo, last, lo))
    landed(14, (first, xo, hi))
    landed(15, (last, xo, hi))
    for copy in hops:
        copy.wait_send()
    own_a.wait()
    rest = recv_ref.at[pl.ds(0, 127)]
    pltpu.make_async_remote_copy(
        rest, rest, main_s, main_r, device_id=(row, col), device_id_type=MESH
    ).wait()


def exchange(send):
    dma = pltpu.SemaphoreType.DMA
    return pl.pallas_call(
        exchange_kernel,
        out_shape=(
            jax.ShapeDtypeStruct((128, BLK, BLK), jnp.float32),
            jax.ShapeDtypeStruct((4, 4, 8, BLK, BLK), jnp.float32),
        ),
        in_specs=[ANY],
        out_specs=(ANY, ANY),
        scratch_shapes=[dma, dma, dma, dma, dma((2,)), dma((16,)), dma((16,))],
        compiler_params=pltpu.CompilerParams(has_side_effects=True),
        name="exchange",
    )(send)


def split(value):
    high = value.astype(jnp.bfloat16)
    return high, (value - high.astype(jnp.float32)).astype(jnp.bfloat16)


def dot1(a, b):
    return jnp.dot(a, b, preferred_element_type=jnp.float32)


def dot3(a, b):
    return dot1(a[0], b[0]) + (dot1(a[0], b[1]) + dot1(a[1], b[0]))


def identity(n):
    return lax.broadcasted_iota(jnp.int32, (n, n), 0) == lax.broadcasted_iota(jnp.int32, (n, n), 1)


def inverse_into(matrix_ref, scaled_ref, x_ref, out_ref):
    eye = identity(PW)
    matrix = matrix_ref[...]
    diagonal = jnp.where(eye, matrix, 0.0)
    by_col = lax.rsqrt(jnp.sum(diagonal, axis=0, keepdims=True))
    by_row = lax.rsqrt(jnp.sum(diagonal, axis=1, keepdims=True))
    scaled = matrix * by_row * by_col
    scaled_ref[...] = scaled
    bound = jnp.max(jnp.sum(jnp.abs(scaled), axis=0, keepdims=True))
    alpha = jnp.minimum(1.0, 1.9 / bound)
    x_ref[...] = jnp.where(eye, 2.0 * alpha, 0.0) - alpha * alpha * scaled

    def body(carry):
        count, _ = carry
        value = split(x_ref[...])
        residual = jnp.where(eye, 1.0, 0.0) - dot3(split(scaled_ref[...]), value)
        x_ref[...] += dot3(value, split(residual))
        return count + 1, jnp.sum(residual * residual)

    lax.while_loop(
        lambda carry: (carry[0] < 48) & (carry[1] > 1e-6), body, (jnp.int32(0), jnp.float32(1.0))
    )
    residual = jnp.where(eye, 1.0, 0.0) - jnp.dot(
        scaled_ref[...], x_ref[...], precision=lax.Precision.HIGHEST, preferred_element_type=jnp.float32
    )
    value = x_ref[...]
    value = value + dot3(split(value), split(residual))
    out_ref[...] = value * by_row * by_col


def pivot_kernel(
    table_ref, diag_ref, recv_ref, strip_ref, y_ref, f_ref,
    strips, blocks, piv, tile, inv0, inv1, l10, scaled, newton, schur, sems,
):
    row, col = lax.axis_index("row"), lax.axis_index("col")

    @pl.when(col == 0)
    def _():
        load_a = pltpu.make_async_copy(strip_ref, strips, sems.at[0])
        load_b = pltpu.make_async_copy(recv_ref, blocks, sems.at[1])
        load_a.start()
        load_b.start()
        load_a.wait()

        def pivot_block(step, carry):
            a, b = step // 8, step % 8
            total = jnp.where(identity(BLK) & (a == b), diag_ref[pl.ds(a, 1), :], 0.0)
            for k in range(2):
                ga, gb = table_ref[k, 24 + a], table_ref[k, 24 + b]
                value = strips[k * 8 + jnp.maximum(ga, 0), jnp.maximum(gb, 0)]
                total = total + jnp.where((ga >= 0) & (gb >= 0), value, 0.0)
            piv[pl.ds(pl.multiple_of(a * BLK, BLK), BLK), pl.ds(pl.multiple_of(b * BLK, BLK), BLK)] = total
            return carry

        lax.fori_loop(0, 64, pivot_block, 0)
        schur[...] = piv[:PW, :PW]
        inverse_into(schur, scaled, newton, inv0)
        l10[...] = dot3(split(piv[PW:, :PW]), split(inv0[...]))
        schur[...] = piv[PW:, PW:] - dot3(split(l10[...]), split(piv[:PW, PW:]))

        load_b.wait()

        @pl.when(row == 0)
        def _():
            f_ref[:PW, :] = piv[:PW, :]
            f_ref[PW:, :PW] = l10[...]
            f_ref[PW:, PW:] = schur[...]
            y_ref[...] = jnp.zeros((TR, TR), jnp.float32)
            y_ref[PW:, :PW] = l10[...]

        @pl.when(row > 0)
        def _():
            inverse_into(schur, scaled, newton, inv1)

            def tile_block(step, carry):
                a, b = step // 8, step % 8
                total = jnp.zeros((BLK, BLK), jnp.float32)
                for k in range(2):
                    ga, hb = table_ref[k, a], table_ref[k, 24 + b]
                    value = blocks[k * 64 + jnp.maximum(ga, 0) * 8 + jnp.maximum(hb, 0)]
                    total = total + jnp.where((ga >= 0) & (hb >= 0), value, 0.0)
                tile[pl.ds(pl.multiple_of(a * BLK, BLK), BLK), pl.ds(pl.multiple_of(b * BLK, BLK), BLK)] = total
                return carry

            lax.fori_loop(0, 64, tile_block, 0)
            for part in range(2):
                rows = pl.ds(part * PW, PW)
                factor0 = dot3(split(tile[rows, :PW]), split(inv0[...]))
                f_ref[rows, :PW] = factor0
                rest = tile[rows, PW:] - dot3(split(factor0), split(piv[:PW, PW:]))
                factor1 = dot3(split(rest), split(inv1[...]))
                f_ref[rows, PW:] = factor1
                y_ref[rows, PW:] = factor1
                y_ref[rows, :PW] = f_ref[rows, :PW] - dot3(split(factor1), split(l10[...]))


def pivots(table, diag, recv, strips):
    f32 = jnp.float32
    half = pltpu.VMEM((PW, PW), f32)
    return pl.pallas_call(
        pivot_kernel,
        out_shape=(jax.ShapeDtypeStruct((TR, TR), f32), jax.ShapeDtypeStruct((TR, TR), f32)),
        in_specs=[SMEM, VMEM, ANY, ANY],
        out_specs=(VMEM, VMEM),
        scratch_shapes=[
            pltpu.VMEM((16, 8, BLK, BLK), f32),
            pltpu.VMEM((128, BLK, BLK), f32),
            pltpu.VMEM((TR, TR), f32),
            pltpu.VMEM((TR, TR), f32),
            half, half, half, half, half, half,
            pltpu.SemaphoreType.DMA((2,)),
        ],
        compiler_params=pltpu.CompilerParams(vmem_limit_bytes=VMEM_LIMIT),
        name="pivots",
    )(table, diag, recv, strips)


CHUNKS = 16


def spread_kernel(y_ref, out_ref, own_sem, ring_s, ring_r, core_s, core_r):
    row, col = lax.axis_index("row"), lax.axis_index("col")
    z, core = col // 2, col % 2
    size = TR // CHUNKS
    own = pltpu.make_async_copy(y_ref, out_ref, own_sem)

    def ring(source, t):
        step = 1 if t % 2 == 0 else 3
        rows = pl.ds(t * size, size)
        return pltpu.make_async_remote_copy(
            source.at[rows], out_ref.at[rows], ring_s.at[t], ring_r.at[t],
            device_id=(row, ((z + step) % 4) * 2), device_id_type=MESH,
        )

    def across(source, t):
        rows = pl.ds(t * size, size)
        return pltpu.make_async_remote_copy(
            source.at[rows], out_ref.at[rows], core_s.at[t], core_r.at[t],
            device_id=(row, z * 2 + 1), device_id_type=MESH,
        )

    @pl.when(col == 0)
    def _():
        own.start()
        for t in range(CHUNKS):
            ring(y_ref, t).start()
        for t in range(CHUNKS):
            across(y_ref, t).start()
        for t in range(CHUNKS):
            ring(y_ref, t).wait_send()
            across(y_ref, t).wait_send()
        own.wait()

    @pl.when((core == 0) & (z > 0))
    def _():
        for t in range(CHUNKS):
            ring(out_ref, t).wait_recv()
            end = 3 if t % 2 == 0 else 1

            @pl.when(z != end)
            def _():
                ring(out_ref, t).start()

            across(out_ref, t).start()
        for t in range(CHUNKS):
            end = 3 if t % 2 == 0 else 1

            @pl.when(z != end)
            def _():
                ring(out_ref, t).wait_send()

            across(out_ref, t).wait_send()

    @pl.when(core == 1)
    def _():
        for t in range(CHUNKS):
            across(out_ref, t).wait_recv()


def spread(y):
    dma = pltpu.SemaphoreType.DMA
    return pl.pallas_call(
        spread_kernel,
        out_shape=jax.ShapeDtypeStruct((TR, TR), jnp.float32),
        in_specs=[ANY],
        out_specs=ANY,
        scratch_shapes=[dma, dma((CHUNKS,)), dma((CHUNKS,)), dma((CHUNKS,)), dma((CHUNKS,))],
        compiler_params=pltpu.CompilerParams(has_side_effects=True),
        name="spread",
    )(y)


def update_kernel(table_ref, diag_ref, y_ref, f_ref, *refs):
    strips, blocks = refs[0:4], refs[4:8]
    out_ref, yh, yl, wh, wl = refs[8:]
    row, col = lax.axis_index("row"), lax.axis_index("col")
    step = pl.program_id(0)

    @pl.when(step == 0)
    def _():
        yh[...], yl[...] = split(y_ref[...])

    for u in range(2):
        j = step * 2 + u

        def strip_block(i, carry):
            on = identity(BLK) & (col * 16 + j == i)
            total = jnp.where(on, diag_ref[pl.ds(i, 1), :], 0.0)
            for k in range(2):
                g, h = table_ref[k, 24 + i], table_ref[k, 8 + j]
                value = strips[2 * u + k][0, 0, jnp.maximum(g, 0)]
                total = total + jnp.where((g >= 0) & (h >= 0), value, 0.0)
            at = pl.ds(pl.multiple_of(i * BLK, BLK), BLK)
            wh[pl.ds(u * BLK, BLK), at], wl[pl.ds(u * BLK, BLK), at] = split(total)
            return carry

        lax.fori_loop(0, 8, strip_block, 0)

    def nt(a, b):
        return lax.dot_general(a, b, (((1,), (1,)), ((), ())), preferred_element_type=jnp.float32)

    for part in range(2):
        rows = pl.ds(part * PW, PW)
        out_ref[rows, :] = -(nt(yh[rows, :], wh[...]) + (nt(yh[rows, :], wl[...]) + nt(yl[rows, :], wh[...])))

    for u in range(2):
        j = step * 2 + u

        def front_block(i, carry):
            on = identity(BLK) & (col * 16 + j == row * 8 + i)
            total = jnp.where(on, diag_ref[pl.ds(row * 8 + i, 1), :], 0.0)
            for k in range(2):
                g, h = table_ref[k, i], table_ref[k, 8 + j]
                value = blocks[2 * u + k][0, jnp.maximum(g, 0), 0]
                total = total + jnp.where((g >= 0) & (h >= 0), value, 0.0)
            out_ref[pl.ds(pl.multiple_of(i * BLK, BLK), BLK), pl.ds(u * BLK, BLK)] += total
            return carry

        lax.fori_loop(0, 8, front_block, 0)

    @pl.when((col == 0) & (step < 4))
    def _():
        out_ref[...] = f_ref[...]


def update(table, diag, y, factors, strips, recv):
    f32, bf16 = jnp.float32, jnp.bfloat16

    def strip_spec(u, k):
        return pl.BlockSpec(
            (1, 1, 8, BLK, BLK),
            lambda s, table: (k, jnp.maximum(table[k, 8 + 2 * s + u], 0), 0, 0, 0),
        )

    def block_spec(u, k):
        return pl.BlockSpec(
            (1, 8, 1, BLK, BLK),
            lambda s, table: (k, 0, jnp.maximum(table[k, 8 + 2 * s + u], 0), 0, 0),
        )

    pairs = [(u, k) for u in range(2) for k in range(2)]
    return pl.pallas_call(
        update_kernel,
        out_shape=jax.ShapeDtypeStruct((TR, TC), f32),
        grid_spec=pltpu.PrefetchScalarGridSpec(
            num_scalar_prefetch=1,
            grid=(8,),
            in_specs=[
                pl.BlockSpec((128, BLK), lambda s, table: (0, 0)),
                pl.BlockSpec((TR, TR), lambda s, table: (0, 0)),
                pl.BlockSpec((TR, 256), lambda s, table: (0, jnp.minimum(s, 3))),
                *[strip_spec(u, k) for u, k in pairs],
                *[block_spec(u, k) for u, k in pairs],
            ],
            out_specs=pl.BlockSpec((TR, 256), lambda s, table: (0, s)),
            scratch_shapes=[
                pltpu.VMEM((TR, TR), bf16),
                pltpu.VMEM((TR, TR), bf16),
                pltpu.VMEM((256, TR), bf16),
                pltpu.VMEM((256, TR), bf16),
            ],
        ),
        compiler_params=pltpu.CompilerParams(vmem_limit_bytes=VMEM_LIMIT),
        name="update",
    )(
        table, diag, y, factors,
        *[strips.reshape(2, 8, 8, BLK, BLK)] * 4,
        *[recv.reshape(2, 8, 8, BLK, BLK)] * 4,
    )


def body(child_blocks, block_map, front_diagonal):
    diag = front_diagonal.reshape(128, BLK)
    send, table = pack(block_map, child_blocks)
    recv, strips = exchange(send)
    strips = strips.reshape(16, 8, BLK, BLK)
    y, factors = pivots(table, diag, recv, strips)
    y = spread(y)
    return update(table, diag, y, factors, strips, recv)


def solution(mesh):
    return jax.shard_map(
        body,
        mesh=mesh,
        in_specs=(P("row", "col"), P(), P()),
        out_specs=P("row", "col"),
        check_vma=False,
    )
```

time: 1090 us -> 564 us (0.52); the launches traced: 1080 us -> 564 us
  Pallas kernels: 0 us -> 564 us
  waiting for transfers between devices: 542 us -> 0 us
  other arithmetic: 289 us -> 0 us
  local copies, waits for them, and re-layouts: 135 us -> 0 us
  matrix products: 75.8 us -> 0 us
  between operations: 19.4 us -> 0.03 us
  starting transfers between devices: 15.1 us -> 0 us
    pallas_call x0 -> x5, Pallas kernels: none -> 564 us  [the longest x1 239 us: spread(): pl.pallas_call(spread_kernel, out_shape=jax.ShapeDtypeStruct((TR, TR), jn...]
    psum x4 -> x0, waiting for transfers between devices: 331 us -> none  [spread(): return lax.psum(kept, axis)]
    another operation x45 -> x0, other arithmetic: 240 us -> none  [the longest x30 159 us: invert(): lower_chol = jnp.linalg.cholesky(normal_matrix)]
    all_to_all x2 -> x0, waiting for transfers between devices: 211 us -> none  [the longest x1 120 us: body(): lax.all_to_all(outgoing, 'row', split_axis=0, concat_axis=0, tiled=True)]
    dot_general x6 -> x0, matrix products: 59.8 us -> none  [the longest x2 40 us: body(): jnp.dot(factor, upper_part, precision=lax.Precision.HIGHEST, preferred_el...]
    gather x11 -> x0, local copies, waits for them, and re-layouts: 50.7 us -> none  [the longest x9 50 us: take_masked(): gathered = jnp.take(blocks, jnp.maximum(slot_table, 0), axis=which_axis)]
    all_to_all x2 -> x0, local copies, waits for them, and re-layouts: 19.9 us -> none  [the longest x1 10.7 us: body(): lax.all_to_all(outgoing, 'col', split_axis=1, concat_axis=1, tiled=True)]
    mul x4 -> x0, other arithmetic: 19.5 us -> none  [take_masked(): gathered * (slot_table >= 0).astype(gathered.dtype).reshape(mask_shape)]
  transfers between devices with their start and end apart: 6 -> 0, of which waited for: 6 -> 0; matrix products, arithmetic and copies ran while one was open for 1% -> 0% of each run, Pallas kernels for 0% -> 0%
where the time goes in v1:
time: 564 us
  Pallas kernels  564 us (100%)
    pallas_call x1, Pallas kernels, spread(): pl.pallas_call(spread_kernel, out_shape=jax.ShapeDtypeStruct((TR, TR), jn...  239 us
    pallas_call x1, Pallas kernels, exchange(): pl.pallas_call(exchange_kernel, out_shape=(jax.ShapeDtypeStruct((128, BLK...  161 us
    pallas_call x1, Pallas kernels, pack(): pl.pallas_call(pack_kernel, out_shape=(jax.ShapeDtypeStruct((64, BLK, BLK...  129 us
    pallas_call x1, Pallas kernels, update(): pl.pallas_call(update_kernel, out_shape=jax.ShapeDtypeStruct((TR, TC), f3...  30.3 us

profile of v1, /device:TPU:33, one launch (start us, length us, event | category | flops | bytes accessed | tf_op | source)
XLA Modules:
  0.0 564.2 jit_solution(14865979653854874959)
XLA Ops:
  0.0 129.5 %pack.1 = (f32[64,128,128]{2,1,0:T(8,128)}, s32[2,32]{1,0:T(2,128)}) custom-call(s32[2,64]{1,0:T(2,128)} %map_ref.1, f32[1024,1024]{1,0:T(8,128)} %child_ref.1), custom_call_target="tpu_custom_call" | custom-call | tf_op jit(solution)/shard_map/pack/pallas_call | solution.py:67
  129.5 160.7 %exchange.1 = (f32[128,128,128]{2,1,0:T(8,128)}, f32[4,4,8,128,128]{4,3,2,1,0:T(8,128)}) custom-call(f32[64,128,128]{2,1,0:T(8,128)} %get-tuple-element.12.send_ref), custom_call_target="tpu_custom_call" | custom-call | tf_op jit(solution)/shard_map/exchange/pallas_call | solution.py:196
  290.2 4.4 pivots.1
  294.6 239.3 %spread.1.y_ref = f32[1024,1024]{1,0:T(8,128)} custom-call(f32[1024,1024]{1,0:T(8,128)} %get-tuple-element.15.y_ref), custom_call_target="tpu_custom_call" | custom-call | tf_op jit(solution)/shard_map/spread/pallas_call | solution.py:408
  533.9 30.3 %update.1 = f32[1024,2048]{1,0:T(8,128)} custom-call(s32[2,32]{1,0:T(2,128)} %get-tuple-element.11.table_ref, f32[128,128]{1,0:T(8,128)} %bitcast.14, f32[1024,1024]{1,0:T(8,128)} %spread.1.y_ref, f32[1024,1024]{1,0:T(8,128)} %get-tuple-element.16.f_ref, f32[2,8,8,128,128]{4,3,2,1,0:T(8,128)} %bitcast.9, f32[2,8,8,128,128]{4,3,2,1,0:T(8,128)} %bitcast.10, ...), custom_call_target="tpu_custom_call" | custom-call | tf_op jit(solution)/shard_map/update/pallas_call | solution.py:488

commit v2 on v1

--- a/solution.py
+++ b/solution.py
@@ -14,6 +14,7 @@
 ANY = pl.BlockSpec(memory_space=pl.ANY)
 SMEM = pl.BlockSpec(memory_space=pltpu.SMEM)
 VMEM = pl.BlockSpec(memory_space=pltpu.VMEM)
+HBM = pl.BlockSpec(memory_space=pltpu.HBM)
 
 
 def pack_kernel(map_ref, child_ref, send_ref, table_ref, sem):
@@ -24,13 +25,10 @@
         t, u = step // 8, step % 8
         q = map_ref[child, group * 8 + t] // 16
         c = map_ref[child, col * 8 + u] // 16
-        pltpu.make_async_copy(
-            child_ref.at[
-                pl.ds(pl.multiple_of(t * BLK, BLK), BLK), pl.ds(pl.multiple_of(u * BLK, BLK), BLK)
-            ],
-            send_ref.at[q * 8 + c],
-            sem,
-        ).start()
+        block = child_ref.at[
+            pl.ds(pl.multiple_of(t * BLK, BLK), BLK), pl.ds(pl.multiple_of(u * BLK, BLK), BLK)
+        ]
+        pltpu.make_async_copy(block, send_ref.at[q * 8 + c], sem).start()
         return carry
 
     lax.fori_loop(0, 64, start, 0)
@@ -70,9 +68,10 @@
             jax.ShapeDtypeStruct((64, BLK, BLK), jnp.float32),
             jax.ShapeDtypeStruct((2, 32), jnp.int32),
         ),
-        in_specs=[SMEM, ANY],
-        out_specs=(ANY, SMEM),
+        in_specs=[SMEM, VMEM],
+        out_specs=(HBM, SMEM),
         scratch_shapes=[pltpu.SemaphoreType.DMA],
+        compiler_params=pltpu.CompilerParams(vmem_limit_bytes=VMEM_LIMIT),
         name="pack",
     )(block_map, child)
 
@@ -85,14 +84,14 @@
     x, y = row % 4, row // 4
 
     own_a = pltpu.make_async_copy(send_ref.at[(row // 2) * 8 + col], recv_ref.at[me], own_sem.at[0])
-    own_b = pltpu.make_async_copy(send_ref.at[col * 8], strip_ref.at[y, x, col], own_sem.at[1])
+    own_b = pltpu.make_async_copy(send_ref.at[col], strip_ref.at[y, x, col], own_sem.at[1])
     own_a.start()
     own_b.start()
 
     def send_strip(step, carry):
         to = (col + step) % 8
         pltpu.make_async_remote_copy(
-            send_ref.at[to * 8], strip_ref.at[y, x, col], col_s, col_r,
+            send_ref.at[to], strip_ref.at[y, x, col], col_s, col_r,
             device_id=(row, to), device_id_type=MESH,
         ).start()
         return carry
@@ -200,7 +199,7 @@
             jax.ShapeDtypeStruct((4, 4, 8, BLK, BLK), jnp.float32),
         ),
         in_specs=[ANY],
-        out_specs=(ANY, ANY),
+        out_specs=(HBM, HBM),
         scratch_shapes=[dma, dma, dma, dma, dma((2,)), dma((16,)), dma((16,))],
         compiler_params=pltpu.CompilerParams(has_side_effects=True),
         name="exchange",
@@ -234,23 +233,42 @@
     scaled_ref[...] = scaled
     bound = jnp.max(jnp.sum(jnp.abs(scaled), axis=0, keepdims=True))
     alpha = jnp.minimum(1.0, 1.9 / bound)
-    x_ref[...] = jnp.where(eye, 2.0 * alpha, 0.0) - alpha * alpha * scaled
-
-    def body(carry):
-        count, _ = carry
-        value = split(x_ref[...])
-        residual = jnp.where(eye, 1.0, 0.0) - dot3(split(scaled_ref[...]), value)
-        x_ref[...] += dot3(value, split(residual))
-        return count + 1, jnp.sum(residual * residual)
-
-    lax.while_loop(
-        lambda carry: (carry[0] < 48) & (carry[1] > 1e-6), body, (jnp.int32(0), jnp.float32(1.0))
-    )
+
+    def begin():
+        x_ref[...] = jnp.where(eye, 2.0 * alpha, 0.0) - alpha * alpha * scaled_ref[...]
+
+    def run(most, settled, first, second):
+        def step(carry):
+            count, _ = carry
+            value = x_ref[...]
+            residual = jnp.where(eye, 1.0, 0.0) - first(scaled_ref[...], value)
+            x_ref[...] += second(value, residual)
+            return count + 1, jnp.sum(residual * residual)
+
+        return lax.while_loop(
+            lambda carry: (carry[0] < most) & (carry[1] > settled), step, (jnp.int32(0), jnp.float32(1e9))
+        )[1]
+
+    def once(a, b):
+        return dot1(a.astype(jnp.bfloat16), b.astype(jnp.bfloat16))
+
+    def thrice(a, b):
+        return dot3(split(a), split(b))
+
+    begin()
+    run(10, 1.0, once, once)
+    left = run(5, 1e-6, thrice, once)
+
+    @pl.when(jnp.logical_not(left <= 1e-6))
+    def _():
+        begin()
+        run(48, 1e-6, thrice, thrice)
+
     residual = jnp.where(eye, 1.0, 0.0) - jnp.dot(
         scaled_ref[...], x_ref[...], precision=lax.Precision.HIGHEST, preferred_element_type=jnp.float32
     )
     value = x_ref[...]
-    value = value + dot3(split(value), split(residual))
+    value = value + thrice(value, residual)
     out_ref[...] = value * by_row * by_col
 
 
@@ -344,11 +362,10 @@
 CHUNKS = 16
 
 
-def spread_kernel(y_ref, out_ref, own_sem, ring_s, ring_r, core_s, core_r):
+def spread_kernel(y_ref, out_ref, ring_s, ring_r, core_s, core_r):
     row, col = lax.axis_index("row"), lax.axis_index("col")
     z, core = col // 2, col % 2
     size = TR // CHUNKS
-    own = pltpu.make_async_copy(y_ref, out_ref, own_sem)
 
     def ring(source, t):
         step = 1 if t % 2 == 0 else 3
@@ -367,35 +384,35 @@
 
     @pl.when(col == 0)
     def _():
-        own.start()
         for t in range(CHUNKS):
+            if t >= 4:
+                ring(y_ref, t - 4).wait_send()
             ring(y_ref, t).start()
-        for t in range(CHUNKS):
             across(y_ref, t).start()
         for t in range(CHUNKS):
-            ring(y_ref, t).wait_send()
+            if t >= CHUNKS - 4:
+                ring(y_ref, t).wait_send()
             across(y_ref, t).wait_send()
-        own.wait()
-
-    @pl.when((core == 0) & (z > 0))
-    def _():
-        for t in range(CHUNKS):
+
+    def relay(place):
+        def due(t):
+            return t // 2 + (place if t % 2 == 0 else 4 - place)
+
+        for t in sorted(range(CHUNKS), key=lambda t: (due(t), t)):
             ring(out_ref, t).wait_recv()
-            end = 3 if t % 2 == 0 else 1
-
-            @pl.when(z != end)
-            def _():
+            if place != (3 if t % 2 == 0 else 1):
                 ring(out_ref, t).start()
-
             across(out_ref, t).start()
         for t in range(CHUNKS):
-            end = 3 if t % 2 == 0 else 1
-
-            @pl.when(z != end)
-            def _():
+            if place != (3 if t % 2 == 0 else 1):
                 ring(out_ref, t).wait_send()
-
             across(out_ref, t).wait_send()
+
+    for place in range(1, 4):
+
+        @pl.when((core == 0) & (z == place))
+        def _(place=place):
+            relay(place)
 
     @pl.when(core == 1)
     def _():
@@ -408,83 +425,88 @@
     return pl.pallas_call(
         spread_kernel,
         out_shape=jax.ShapeDtypeStruct((TR, TR), jnp.float32),
-        in_specs=[ANY],
-        out_specs=ANY,
-        scratch_shapes=[dma, dma((CHUNKS,)), dma((CHUNKS,)), dma((CHUNKS,)), dma((CHUNKS,))],
+        in_specs=[HBM],
+        out_specs=HBM,
+        scratch_shapes=[dma((CHUNKS,)), dma((CHUNKS,)), dma((CHUNKS,)), dma((CHUNKS,))],
         compiler_params=pltpu.CompilerParams(has_side_effects=True),
         name="spread",
     )(y)
 
 
-def update_kernel(table_ref, diag_ref, y_ref, f_ref, *refs):
+def update_kernel(table_ref, diag_ref, f_ref, own_ref, came_ref, *refs):
     strips, blocks = refs[0:4], refs[4:8]
-    out_ref, yh, yl, wh, wl = refs[8:]
+    out_ref, y, yh, yl, uh, ul, sem = refs[8:]
     row, col = lax.axis_index("row"), lax.axis_index("col")
     step = pl.program_id(0)
 
     @pl.when(step == 0)
     def _():
-        yh[...], yl[...] = split(y_ref[...])
-
-    for u in range(2):
-        j = step * 2 + u
-
-        def strip_block(i, carry):
-            on = identity(BLK) & (col * 16 + j == i)
-            total = jnp.where(on, diag_ref[pl.ds(i, 1), :], 0.0)
-            for k in range(2):
-                g, h = table_ref[k, 24 + i], table_ref[k, 8 + j]
-                value = strips[2 * u + k][0, 0, jnp.maximum(g, 0)]
-                total = total + jnp.where((g >= 0) & (h >= 0), value, 0.0)
-            at = pl.ds(pl.multiple_of(i * BLK, BLK), BLK)
-            wh[pl.ds(u * BLK, BLK), at], wl[pl.ds(u * BLK, BLK), at] = split(total)
-            return carry
-
-        lax.fori_loop(0, 8, strip_block, 0)
-
-    def nt(a, b):
-        return lax.dot_general(a, b, (((1,), (1,)), ((), ())), preferred_element_type=jnp.float32)
-
-    for part in range(2):
-        rows = pl.ds(part * PW, PW)
-        out_ref[rows, :] = -(nt(yh[rows, :], wh[...]) + (nt(yh[rows, :], wl[...]) + nt(yl[rows, :], wh[...])))
-
-    for u in range(2):
-        j = step * 2 + u
-
-        def front_block(i, carry):
-            on = identity(BLK) & (col * 16 + j == row * 8 + i)
-            total = jnp.where(on, diag_ref[pl.ds(row * 8 + i, 1), :], 0.0)
-            for k in range(2):
-                g, h = table_ref[k, i], table_ref[k, 8 + j]
-                value = blocks[2 * u + k][0, jnp.maximum(g, 0), 0]
-                total = total + jnp.where((g >= 0) & (h >= 0), value, 0.0)
-            out_ref[pl.ds(pl.multiple_of(i * BLK, BLK), BLK), pl.ds(u * BLK, BLK)] += total
-            return carry
-
-        lax.fori_loop(0, 8, front_block, 0)
-
-    @pl.when((col == 0) & (step < 4))
+        @pl.when(col == 0)
+        def _():
+            copy = pltpu.make_async_copy(own_ref, y, sem)
+            copy.start()
+            copy.wait()
+
+        @pl.when(col != 0)
+        def _():
+            copy = pltpu.make_async_copy(came_ref, y, sem)
+            copy.start()
+            copy.wait()
+
+        yh[...], yl[...] = split(y[...])
+
+    factors = (col == 0) & (step < 4)
+
+    @pl.when(factors)
     def _():
         out_ref[...] = f_ref[...]
 
-
-def update(table, diag, y, factors, strips, recv):
+    @pl.when(jnp.logical_not(factors))
+    def _():
+        for u in range(2):
+            j = step * 2 + u
+
+            def strip_block(i, carry):
+                on = identity(BLK) & (col * 16 + j == i)
+                total = jnp.where(on, diag_ref[pl.ds(i, 1), :], 0.0)
+                for k in range(2):
+                    g, h = table_ref[k, 24 + i], table_ref[k, 8 + j]
+                    value = strips[2 * u + k][0, jnp.maximum(g, 0), 0]
+                    total = total + jnp.where((g >= 0) & (h >= 0), value, 0.0)
+                at = pl.ds(pl.multiple_of(i * BLK, BLK), BLK)
+                uh[at, pl.ds(u * BLK, BLK)], ul[at, pl.ds(u * BLK, BLK)] = split(total)
+                return carry
+
+            lax.fori_loop(0, 8, strip_block, 0)
+
+        out_ref[...] = dot3((yh[...], yl[...]), (uh[...], ul[...]))
+        for u in range(2):
+            j = step * 2 + u
+
+            def front_block(i, carry):
+                on = identity(BLK) & (col * 16 + j == row * 8 + i)
+                total = jnp.where(on, diag_ref[pl.ds(row * 8 + i, 1), :], 0.0)
+                for k in range(2):
+                    g, h = table_ref[k, i], table_ref[k, 8 + j]
+                    value = blocks[2 * u + k][0, jnp.maximum(g, 0), 0]
+                    total = total + jnp.where((g >= 0) & (h >= 0), value, 0.0)
+                at = pl.ds(pl.multiple_of(i * BLK, BLK), BLK), pl.ds(u * BLK, BLK)
+                out_ref[at] = total - out_ref[at]
+                return carry
+
+            lax.fori_loop(0, 8, front_block, 0)
+
+
+def update(table, diag, factors, own, came, strips, recv):
     f32, bf16 = jnp.float32, jnp.bfloat16
 
-    def strip_spec(u, k):
-        return pl.BlockSpec(
-            (1, 1, 8, BLK, BLK),
-            lambda s, table: (k, jnp.maximum(table[k, 8 + 2 * s + u], 0), 0, 0, 0),
-        )
-
-    def block_spec(u, k):
+    def spec(u, k):
         return pl.BlockSpec(
             (1, 8, 1, BLK, BLK),
             lambda s, table: (k, 0, jnp.maximum(table[k, 8 + 2 * s + u], 0), 0, 0),
         )
 
-    pairs = [(u, k) for u in range(2) for k in range(2)]
+    column_specs = [spec(u, k) for u in range(2) for k in range(2)]
     return pl.pallas_call(
         update_kernel,
         out_shape=jax.ShapeDtypeStruct((TR, TC), f32),
@@ -493,23 +515,26 @@
             grid=(8,),
             in_specs=[
                 pl.BlockSpec((128, BLK), lambda s, table: (0, 0)),
-                pl.BlockSpec((TR, TR), lambda s, table: (0, 0)),
                 pl.BlockSpec((TR, 256), lambda s, table: (0, jnp.minimum(s, 3))),
-                *[strip_spec(u, k) for u, k in pairs],
-                *[block_spec(u, k) for u, k in pairs],
+                HBM,
+                HBM,
+                *column_specs,
+                *column_specs,
             ],
             out_specs=pl.BlockSpec((TR, 256), lambda s, table: (0, s)),
             scratch_shapes=[
+                pltpu.VMEM((TR, TR), f32),
                 pltpu.VMEM((TR, TR), bf16),
                 pltpu.VMEM((TR, TR), bf16),
-                pltpu.VMEM((256, TR), bf16),
-                pltpu.VMEM((256, TR), bf16),
+                pltpu.VMEM((TR, 256), bf16),
+                pltpu.VMEM((TR, 256), bf16),
+                pltpu.SemaphoreType.DMA,
             ],
         ),
         compiler_params=pltpu.CompilerParams(vmem_limit_bytes=VMEM_LIMIT),
         name="update",
     )(
-        table, diag, y, factors,
+        table, diag, factors, own, came,
         *[strips.reshape(2, 8, 8, BLK, BLK)] * 4,
         *[recv.reshape(2, 8, 8, BLK, BLK)] * 4,
     )
@@ -521,8 +546,8 @@
     recv, strips = exchange(send)
     strips = strips.reshape(16, 8, BLK, BLK)
     y, factors = pivots(table, diag, recv, strips)
-    y = spread(y)
-    return update(table, diag, y, factors, strips, recv)
+    came = spread(y)
+    return update(table, diag, factors, y, came, strips, recv)
 
 
 def solution(mesh):

time: 564 us -> 299 us (0.53)
  Pallas kernels: 564 us -> 299 us
    pallas_call x1, Pallas kernels: 239 us -> 93.4 us  [spread(): pl.pallas_call(spread_kernel, out_shape=jax.ShapeDtypeStruct((TR, TR), jn...]
    pallas_call x1, Pallas kernels: 129 us -> 9.02 us  [pack(): pl.pallas_call(pack_kernel, out_shape=(jax.ShapeDtypeStruct((64, BLK, BLK...]
where the time goes in v2:
time: 299 us
  Pallas kernels  299 us (100%)
    pallas_call x1, Pallas kernels, exchange(): pl.pallas_call(exchange_kernel, out_shape=(jax.ShapeDtypeStruct((128, BLK...  161 us
    pallas_call x1, Pallas kernels, spread(): pl.pallas_call(spread_kernel, out_shape=jax.ShapeDtypeStruct((TR, TR), jn...  93.4 us
    pallas_call x1, Pallas kernels, update(): pl.pallas_call(update_kernel, out_shape=jax.ShapeDtypeStruct((TR, TC), f3...  31.2 us
    pallas_call x1, Pallas kernels, pack(): pl.pallas_call(pack_kernel, out_shape=(jax.ShapeDtypeStruct((64, BLK, BLK...  9.02 us

profile of v2, /device:TPU:33, one launch (start us, length us, event | category | flops | bytes accessed | tf_op | source)
XLA Modules:
  0.0 298.9 jit_solution(5060850403029220538)
XLA Ops:
  0.0 9.0 %pack.1 = (f32[64,128,128]{2,1,0:T(8,128)}, s32[2,32]{1,0:T(2,128)}) custom-call(s32[2,64]{1,0:T(2,128)} %map_ref.1, f32[1024,1024]{1,0:T(8,128)} %child_ref.1), custom_call_target="tpu_custom_call" | custom-call | tf_op jit(solution)/shard_map/pack/pallas_call | solution.py:65
  9.0 160.7 %exchange.1 = (f32[128,128,128]{2,1,0:T(8,128)}, f32[4,4,8,128,128]{4,3,2,1,0:T(8,128)}) custom-call(f32[64,128,128]{2,1,0:T(8,128)} %get-tuple-element.12.send_ref), custom_call_target="tpu_custom_call" | custom-call | tf_op jit(solution)/shard_map/exchange/pallas_call | solution.py:195
  169.8 4.3 %pivots.1 = (f32[1024,1024]{1,0:T(8,128)}, f32[1024,1024]{1,0:T(8,128)}) custom-call(s32[2,32]{1,0:T(2,128)} %get-tuple-element.11.table_ref, f32[128,128]{1,0:T(8,128)} %bitcast.13, f32[128,128,128]{2,1,0:T(8,128)} %get-tuple-element.13.recv_ref, f32[16,8,128,128]{3,2,1,0:T(8,128)} %bitcast.8), custom_call_target="tpu_custom_call" | custom-call | tf_op jit(solution)/shard_map/pivots/pallas_call | solution.py:344
  174.1 93.4 %spread.1.came_ref = f32[1024,1024]{1,0:T(8,128)} custom-call(f32[1024,1024]{1,0:T(8,128)} %get-tuple-element.16.y_ref.own_ref), custom_call_target="tpu_custom_call" | custom-call | tf_op jit(solution)/shard_map/spread/pallas_call | solution.py:425
  267.5 31.2 %update.1 = f32[1024,2048]{1,0:T(8,128)} custom-call(s32[2,32]{1,0:T(2,128)} %get-tuple-element.11.table_ref, f32[128,128]{1,0:T(8,128)} %bitcast.14, f32[1024,1024]{1,0:T(8,128)} %get-tuple-element.15.f_ref, f32[1024,1024]{1,0:T(8,128)} %get-tuple-element.16.y_ref.own_ref, f32[1024,1024]{1,0:T(8,128)} %spread.1.came_ref, f32[2,8,8,128,128]{4,3,2,1,0:T(8,128)} %bitcast.9, ...), custom_call_target="tpu_custom_call" | custom-call | tf_op jit(solution)/shard_map/update/pallas_call | solution.py:510

commit v3 on v2

--- a/solution.py
+++ b/solution.py
@@ -7,6 +7,8 @@
 
 BLK = 128
 PW = 512
+TOP = 80
+BOT = BLK - TOP
 TR = 1024
 TC = 2048
 MESH = pl.DeviceIdType.MESH
@@ -17,7 +19,7 @@
 HBM = pl.BlockSpec(memory_space=pltpu.HBM)
 
 
-def pack_kernel(map_ref, child_ref, send_ref, table_ref, sem):
+def pack_kernel(map_ref, child_ref, send_ref, rest_ref, table_ref, sem, rest_sem):
     row, col = lax.axis_index("row"), lax.axis_index("col")
     child, group = row // 8, row % 8
 
@@ -29,6 +31,11 @@
             pl.ds(pl.multiple_of(t * BLK, BLK), BLK), pl.ds(pl.multiple_of(u * BLK, BLK), BLK)
         ]
         pltpu.make_async_copy(block, send_ref.at[q * 8 + c], sem).start()
+        rest = child_ref.at[
+            pl.ds(pl.multiple_of(t * BLK + TOP, 16), BOT), pl.ds(pl.multiple_of(u * BLK, BLK), BLK)
+        ]
+        pltpu.make_async_copy(rest, rest_ref.at[q * 16 + c], rest_sem).start()
+        pltpu.make_async_copy(rest, rest_ref.at[q * 16 + 8 + c], rest_sem).start()
         return carry
 
     lax.fori_loop(0, 64, start, 0)
@@ -58,7 +65,13 @@
         return carry
 
     lax.fori_loop(0, 128, look, 0)
+    for k in range(2):
+        for j in range(16):
+            here = table_ref[k, 8 + j]
+            before = table_ref[k, 32 + j - 2] if j >= 2 else 0
+            table_ref[k, 32 + j] = jnp.where(here >= 0, here, before)
     pltpu.make_async_copy(send_ref, send_ref, sem).wait()
+    pltpu.make_async_copy(rest_ref, rest_ref, rest_sem).wait()
 
 
 def pack(block_map, child):
@@ -66,26 +79,36 @@
         pack_kernel,
         out_shape=(
             jax.ShapeDtypeStruct((64, BLK, BLK), jnp.float32),
-            jax.ShapeDtypeStruct((2, 32), jnp.int32),
+            jax.ShapeDtypeStruct((128, BOT, BLK), jnp.float32),
+            jax.ShapeDtypeStruct((2, 48), jnp.int32),
         ),
         in_specs=[SMEM, VMEM],
-        out_specs=(HBM, SMEM),
-        scratch_shapes=[pltpu.SemaphoreType.DMA],
+        out_specs=(HBM, HBM, SMEM),
+        scratch_shapes=[pltpu.SemaphoreType.DMA, pltpu.SemaphoreType.DMA],
         compiler_params=pltpu.CompilerParams(vmem_limit_bytes=VMEM_LIMIT),
         name="pack",
     )(block_map, child)
 
 
 def exchange_kernel(
-    send_ref, recv_ref, strip_ref, main_s, main_r, col_s, col_r, own_sem, gat_s, gat_r
+    send_ref, recv_ref, left_ref, strip_ref,
+    main_s, main_r, left_s, left_r, col_s, col_r, own_sem, gat_s, gat_r,
 ):
     row, col = lax.axis_index("row"), lax.axis_index("col")
     me = row * 8 + col
     x, y = row % 4, row // 4
 
-    own_a = pltpu.make_async_copy(send_ref.at[(row // 2) * 8 + col], recv_ref.at[me], own_sem.at[0])
+    top, bottom = pl.ds(0, TOP), pl.ds(TOP, BOT)
+    own = send_ref.at[(row // 2) * 8]
+    own_a = pltpu.make_async_copy(own.at[top], recv_ref.at[me], own_sem.at[0])
+    own_c = pltpu.make_async_copy(own.at[bottom], left_ref.at[me], own_sem.at[2])
     own_b = pltpu.make_async_copy(send_ref.at[col], strip_ref.at[y, x, col], own_sem.at[1])
-    own_a.start()
+
+    @pl.when(col == 0)
+    def _():
+        own_a.start()
+        own_c.start()
+
     own_b.start()
 
     def send_strip(step, carry):
@@ -101,10 +124,22 @@
     def send_block(step, carry):
         to = (me + step * 45) % 128
         to_row, to_col = to // 8, to % 8
-        pltpu.make_async_remote_copy(
-            send_ref.at[(to_row // 2) * 8 + to_col], recv_ref.at[me], main_s, main_r,
-            device_id=(to_row, to_col), device_id_type=MESH,
-        ).start()
+        block = send_ref.at[(to_row // 2) * 8 + to_col]
+
+        @pl.when((to_col == 0) | (to_col // 2 != col // 2))
+        def _():
+            pltpu.make_async_remote_copy(
+                block.at[top], recv_ref.at[me], main_s, main_r,
+                device_id=(to_row, to_col), device_id_type=MESH,
+            ).start()
+
+        @pl.when(to_col == 0)
+        def _():
+            pltpu.make_async_remote_copy(
+                block.at[bottom], left_ref.at[me], left_s, left_r,
+                device_id=(to_row, to_col), device_id_type=MESH,
+            ).start()
+
         return carry
 
     xp, xm = y * 4 + (x + 1) % 4, y * 4 + (x + 3) % 4
@@ -183,11 +218,34 @@
     landed(15, (last, xo, hi))
     for copy in hops:
         copy.wait_send()
-    own_a.wait()
-    rest = recv_ref.at[pl.ds(0, 127)]
-    pltpu.make_async_remote_copy(
-        rest, rest, main_s, main_r, device_id=(row, col), device_id_type=MESH
-    ).wait()
+
+    def blocks(ref, count, send_sem, recv_sem):
+        part = ref.at[pl.ds(0, count)]
+        return pltpu.make_async_remote_copy(
+            part, part, send_sem, recv_sem, device_id=(row, col), device_id_type=MESH
+        )
+
+    @pl.when(col == 0)
+    def _():
+        own_a.wait()
+        own_c.wait()
+        blocks(recv_ref, 111, main_s, main_r).wait_send()
+        blocks(left_ref, 15, left_s, left_r).wait_send()
+        blocks(recv_ref, 127, main_s, main_r).wait_recv()
+        blocks(left_ref, 127, left_s, left_r).wait_recv()
+
+    @pl.when(col == 1)
+    def _():
+        blocks(recv_ref, 112, main_s, main_r).wait_send()
+
+    @pl.when(col > 1)
+    def _():
+        blocks(recv_ref, 96, main_s, main_r).wait_send()
+
+    @pl.when(col > 0)
+    def _():
+        blocks(left_ref, 16, left_s, left_r).wait_send()
+        blocks(recv_ref, 96, main_s, main_r).wait_recv()
 
 
 def exchange(send):
@@ -195,13 +253,14 @@
     return pl.pallas_call(
         exchange_kernel,
         out_shape=(
-            jax.ShapeDtypeStruct((128, BLK, BLK), jnp.float32),
+            jax.ShapeDtypeStruct((128, TOP, BLK), jnp.float32),
+            jax.ShapeDtypeStruct((128, BOT, BLK), jnp.float32),
             jax.ShapeDtypeStruct((4, 4, 8, BLK, BLK), jnp.float32),
         ),
-        in_specs=[ANY],
-        out_specs=(HBM, HBM),
-        scratch_shapes=[dma, dma, dma, dma, dma((2,)), dma((16,)), dma((16,))],
-        compiler_params=pltpu.CompilerParams(has_side_effects=True),
+        in_specs=[HBM],
+        out_specs=(HBM, HBM, HBM),
+        scratch_shapes=[dma, dma, dma, dma, dma, dma, dma((3,)), dma((16,)), dma((16,))],
+        compiler_params=pltpu.CompilerParams(has_side_effects=True, vmem_limit_bytes=VMEM_LIMIT),
         name="exchange",
     )(send)
 
@@ -273,7 +332,7 @@
 
 
 def pivot_kernel(
-    table_ref, diag_ref, recv_ref, strip_ref, y_ref, f_ref,
+    table_ref, diag_ref, recv_ref, left_ref, strip_ref, y_ref, f_ref,
     strips, blocks, piv, tile, inv0, inv1, l10, scaled, newton, schur, sems,
 ):
     row, col = lax.axis_index("row"), lax.axis_index("col")
@@ -281,9 +340,11 @@
     @pl.when(col == 0)
     def _():
         load_a = pltpu.make_async_copy(strip_ref, strips, sems.at[0])
-        load_b = pltpu.make_async_copy(recv_ref, blocks, sems.at[1])
+        load_b = pltpu.make_async_copy(recv_ref, blocks.at[:, pl.ds(0, TOP)], sems.at[1])
+        load_c = pltpu.make_async_copy(left_ref, blocks.at[:, pl.ds(TOP, BOT)], sems.at[2])
         load_a.start()
         load_b.start()
+        load_c.start()
         load_a.wait()
 
         def pivot_block(step, carry):
@@ -303,6 +364,7 @@
         schur[...] = piv[PW:, PW:] - dot3(split(l10[...]), split(piv[:PW, PW:]))
 
         load_b.wait()
+        load_c.wait()
 
         @pl.when(row == 0)
         def _():
@@ -338,13 +400,13 @@
                 y_ref[rows, :PW] = f_ref[rows, :PW] - dot3(split(factor1), split(l10[...]))
 
 
-def pivots(table, diag, recv, strips):
+def pivots(table, diag, recv, left, strips):
     f32 = jnp.float32
     half = pltpu.VMEM((PW, PW), f32)
     return pl.pallas_call(
         pivot_kernel,
         out_shape=(jax.ShapeDtypeStruct((TR, TR), f32), jax.ShapeDtypeStruct((TR, TR), f32)),
-        in_specs=[SMEM, VMEM, ANY, ANY],
+        in_specs=[SMEM, VMEM, HBM, HBM, HBM],
         out_specs=(VMEM, VMEM),
         scratch_shapes=[
             pltpu.VMEM((16, 8, BLK, BLK), f32),
@@ -352,18 +414,21 @@
             pltpu.VMEM((TR, TR), f32),
             pltpu.VMEM((TR, TR), f32),
             half, half, half, half, half, half,
-            pltpu.SemaphoreType.DMA((2,)),
+            pltpu.SemaphoreType.DMA((3,)),
         ],
         compiler_params=pltpu.CompilerParams(vmem_limit_bytes=VMEM_LIMIT),
         name="pivots",
-    )(table, diag, recv, strips)
+    )(table, diag, recv, left, strips)
 
 
 CHUNKS = 16
 
 
-def spread_kernel(y_ref, out_ref, ring_s, ring_r, core_s, core_r):
+def spread_kernel(
+    y_ref, send_ref, _, out_ref, recv_ref, ring_s, ring_r, core_s, core_r, flat_s, flat_r, own_sem
+):
     row, col = lax.axis_index("row"), lax.axis_index("col")
+    me = row * 8 + col
     z, core = col // 2, col % 2
     size = TR // CHUNKS
 
@@ -382,6 +447,33 @@
             device_id=(row, z * 2 + 1), device_id_type=MESH,
         )
 
+    def flat(step, carry):
+        to = (row * 2 + core + step * 11) % 32
+        to_row, to_col = to // 2, z * 2 + to % 2
+
+        @pl.when(to_col != 0)
+        def _():
+            pltpu.make_async_remote_copy(
+                send_ref.at[(to_row // 2) * 8 + to_col, pl.ds(0, TOP)], recv_ref.at[me], flat_s, flat_r,
+                device_id=(to_row, to_col), device_id_type=MESH,
+            ).start()
+
+        return carry
+
+    def flats(count):
+        part = recv_ref.at[pl.ds(0, count)]
+        return pltpu.make_async_remote_copy(
+            part, part, flat_s, flat_r, device_id=(row, col), device_id_type=MESH
+        )
+
+    own = pltpu.make_async_copy(
+        send_ref.at[(row // 2) * 8 + col, pl.ds(0, TOP)], recv_ref.at[me], own_sem
+    )
+
+    @pl.when(col != 0)
+    def _():
+        own.start()
+
     @pl.when(col == 0)
     def _():
         for t in range(CHUNKS):
@@ -389,22 +481,25 @@
                 ring(y_ref, t - 4).wait_send()
             ring(y_ref, t).start()
             across(y_ref, t).start()
+            lax.fori_loop(max(2 * t, 1), 2 * t + 2, flat, 0)
         for t in range(CHUNKS):
             if t >= CHUNKS - 4:
                 ring(y_ref, t).wait_send()
             across(y_ref, t).wait_send()
 
     def relay(place):
-        def due(t):
-            return t // 2 + (place if t % 2 == 0 else 4 - place)
-
-        for t in sorted(range(CHUNKS), key=lambda t: (due(t), t)):
+        def goes(t):
+            return place != (3 if t % 2 == 0 else 1)
+
+        order = sorted(range(CHUNKS), key=lambda t: (not goes(t), t))
+        for n, t in enumerate(order):
             ring(out_ref, t).wait_recv()
-            if place != (3 if t % 2 == 0 else 1):
+            if goes(t):
                 ring(out_ref, t).start()
             across(out_ref, t).start()
+            lax.fori_loop(max(2 * n, 1), 2 * n + 2, flat, 0)
         for t in range(CHUNKS):
-            if place != (3 if t % 2 == 0 else 1):
+            if goes(t):
                 ring(out_ref, t).wait_send()
             across(out_ref, t).wait_send()
 
@@ -416,26 +511,50 @@
 
     @pl.when(core == 1)
     def _():
+        lax.fori_loop(1, 32, flat, 0)
         for t in range(CHUNKS):
             across(out_ref, t).wait_recv()
 
-
-def spread(y):
+    @pl.when(col == 0)
+    def _():
+        flats(16).wait_send()
+
+    @pl.when(col == 1)
+    def _():
+        flats(15).wait_send()
+
+    @pl.when(col > 1)
+    def _():
+        flats(31).wait_send()
+
+    @pl.when(col != 0)
+    def _():
+        flats(31).wait_recv()
+        own.wait()
+
+
+def spread(y, send, recv):
     dma = pltpu.SemaphoreType.DMA
     return pl.pallas_call(
         spread_kernel,
-        out_shape=jax.ShapeDtypeStruct((TR, TR), jnp.float32),
-        in_specs=[HBM],
-        out_specs=HBM,
-        scratch_shapes=[dma((CHUNKS,)), dma((CHUNKS,)), dma((CHUNKS,)), dma((CHUNKS,))],
-        compiler_params=pltpu.CompilerParams(has_side_effects=True),
+        out_shape=(
+            jax.ShapeDtypeStruct((TR, TR), jnp.float32),
+            jax.ShapeDtypeStruct((128, TOP, BLK), jnp.float32),
+        ),
+        in_specs=[HBM, HBM, HBM],
+        out_specs=(HBM, HBM),
+        input_output_aliases={2: 1},
+        scratch_shapes=[
+            dma((CHUNKS,)), dma((CHUNKS,)), dma((CHUNKS,)), dma((CHUNKS,)), dma, dma, dma,
+        ],
+        compiler_params=pltpu.CompilerParams(has_side_effects=True, vmem_limit_bytes=VMEM_LIMIT),
         name="spread",
-    )(y)
+    )(y, send, recv)
 
 
 def update_kernel(table_ref, diag_ref, f_ref, own_ref, came_ref, *refs):
-    strips, blocks = refs[0:4], refs[4:8]
-    out_ref, y, yh, yl, uh, ul, sem = refs[8:]
+    strips, tops, bottoms = refs[0:4], refs[4:8], refs[8:12]
+    out_ref, y, yh, yl, uh, ul, sem = refs[12:]
     row, col = lax.axis_index("row"), lax.axis_index("col")
     step = pl.program_id(0)
 
@@ -484,29 +603,34 @@
             j = step * 2 + u
 
             def front_block(i, carry):
-                on = identity(BLK) & (col * 16 + j == row * 8 + i)
-                total = jnp.where(on, diag_ref[pl.ds(row * 8 + i, 1), :], 0.0)
-                for k in range(2):
-                    g, h = table_ref[k, i], table_ref[k, 8 + j]
-                    value = blocks[2 * u + k][0, jnp.maximum(g, 0), 0]
-                    total = total + jnp.where((g >= 0) & (h >= 0), value, 0.0)
-                at = pl.ds(pl.multiple_of(i * BLK, BLK), BLK), pl.ds(u * BLK, BLK)
-                out_ref[at] = total - out_ref[at]
+                for refs, first, count in ((tops, 0, TOP), (bottoms, TOP, BOT)):
+                    there = lax.broadcasted_iota(jnp.int32, (count, BLK), 0) + first
+                    on = (there == lax.broadcasted_iota(jnp.int32, (count, BLK), 1)) & (
+                        col * 16 + j == row * 8 + i
+                    )
+                    total = jnp.where(on, diag_ref[pl.ds(row * 8 + i, 1), :], 0.0)
+                    for k in range(2):
+                        g, h = table_ref[k, i], table_ref[k, 8 + j]
+                        value = refs[2 * u + k][0, jnp.maximum(g, 0), 0]
+                        total = total + jnp.where((g >= 0) & (h >= 0), value, 0.0)
+                    at = pl.ds(pl.multiple_of(i * BLK + first, 16), count), pl.ds(u * BLK, BLK)
+                    out_ref[at] = total - out_ref[at]
                 return carry
 
             lax.fori_loop(0, 8, front_block, 0)
 
 
-def update(table, diag, factors, own, came, strips, recv):
+def update(table, diag, factors, own, came, strips, recv, rest):
     f32, bf16 = jnp.float32, jnp.bfloat16
 
-    def spec(u, k):
-        return pl.BlockSpec(
-            (1, 8, 1, BLK, BLK),
-            lambda s, table: (k, 0, jnp.maximum(table[k, 8 + 2 * s + u], 0), 0, 0),
-        )
-
-    column_specs = [spec(u, k) for u in range(2) for k in range(2)]
+    def specs(rows):
+        def spec(u, k):
+            return pl.BlockSpec(
+                (1, 8, 1, rows, BLK), lambda s, table: (k, 0, table[k, 32 + 2 * s + u], 0, 0)
+            )
+
+        return [spec(u, k) for u in range(2) for k in range(2)]
+
     return pl.pallas_call(
         update_kernel,
         out_shape=jax.ShapeDtypeStruct((TR, TC), f32),
@@ -518,8 +642,9 @@
                 pl.BlockSpec((TR, 256), lambda s, table: (0, jnp.minimum(s, 3))),
                 HBM,
                 HBM,
-                *column_specs,
-                *column_specs,
+                *specs(BLK),
+                *specs(TOP),
+                *specs(BOT),
             ],
             out_specs=pl.BlockSpec((TR, 256), lambda s, table: (0, s)),
             scratch_shapes=[
@@ -536,18 +661,21 @@
     )(
         table, diag, factors, own, came,
         *[strips.reshape(2, 8, 8, BLK, BLK)] * 4,
-        *[recv.reshape(2, 8, 8, BLK, BLK)] * 4,
+        *[recv.reshape(2, 8, 8, TOP, BLK)] * 4,
+        *[rest.reshape(2, 8, 8, BOT, BLK)] * 4,
     )
 
 
 def body(child_blocks, block_map, front_diagonal):
     diag = front_diagonal.reshape(128, BLK)
-    send, table = pack(block_map, child_blocks)
-    recv, strips = exchange(send)
+    send, rest, table = pack(block_map, child_blocks)
+    recv, left, strips = exchange(send)
+    rest, recv, left, strips = lax.optimization_barrier((rest, recv, left, strips))
+    rest = lax.all_to_all(rest, ("row", "col"), split_axis=0, concat_axis=0, tiled=True)
     strips = strips.reshape(16, 8, BLK, BLK)
-    y, factors = pivots(table, diag, recv, strips)
-    came = spread(y)
-    return update(table, diag, factors, y, came, strips, recv)
+    y, factors = pivots(table, diag, recv, left, strips)
+    came, recv = spread(y, send, recv)
+    return update(table, diag, factors, y, came, strips, recv, rest)
 
 
 def solution(mesh):

time: 299 us -> 267 us (0.89)
  Pallas kernels: 299 us -> 250 us
  starting transfers between devices: 0 us -> 12.9 us
    pallas_call x2, Pallas kernels: 254 us -> 204 us  [the longest x1 122 us: exchange(): pl.pallas_call(exchange_kernel, out_shape=(jax.ShapeDtypeStruct((128, TOP...]
    all_to_all x0 -> x1, starting transfers between devices: none -> 12.9 us  [body(): lax.all_to_all(rest, ('row', 'col'), split_axis=0, concat_axis=0, tiled=T...]
  transfers between devices with their start and end apart: 0 -> 1, of which waited for: 0 -> 0; matrix products, arithmetic and copies ran while one was open for 0% -> 0% of each run, Pallas kernels for 0% -> 33%
where the time goes in v3:
time: 267 us; the launch traced here: 265 us
  Pallas kernels  250 us (94%)
  starting transfers between devices  12.9 us (5%)
    pallas_call x1, Pallas kernels, exchange(): pl.pallas_call(exchange_kernel, out_shape=(jax.ShapeDtypeStruct((128, TOP...  122 us
    pallas_call x1, Pallas kernels, spread(): pl.pallas_call(spread_kernel, out_shape=(jax.ShapeDtypeStruct((TR, TR), j...  82.6 us
    pallas_call x1, Pallas kernels, update(): pl.pallas_call(update_kernel, out_shape=jax.ShapeDtypeStruct((TR, TC), f3...  32.3 us
    all_to_all x1, starting transfers between devices, body(): lax.all_to_all(rest, ('row', 'col'), split_axis=0, concat_axis=0, tiled=T...  12.9 us
    pallas_call x1, Pallas kernels, pack(): pl.pallas_call(pack_kernel, out_shape=(jax.ShapeDtypeStruct((64, BLK, BLK...  9.3 us
  transfers between devices with their start and end apart: 1, of which 0 were waited for; matrix products, arithmetic and copies ran while one was open for 0% of the time, Pallas kernels for 33%

profile of v3, /device:TPU:33, one launch (start us, length us, event | category | flops | bytes accessed | tf_op | source)
XLA Modules:
  0.0 264.9 jit_solution(8111626388197007990)
XLA Ops:
  0.0 9.3 %pack.1 = (f32[64,128,128]{2,1,0:T(8,128)}, f32[128,48,128]{2,1,0:T(8,128)}, s32[2,48]{1,0:T(2,128)}) custom-call(s32[2,64]{1,0:T(2,128)} %map_ref.1, f32[1024,1024]{1,0:T(8,128)} %child_ref.1), custom_call_target="tpu_custom_call" | custom-call | tf_op jit(solution)/shard_map/pack/pallas_call | solution.py:78
  9.3 121.6 %exchange.1 = (f32[128,80,128]{2,1,0:T(8,128)}, f32[128,48,128]{2,1,0:T(8,128)}, f32[4,4,8,128,128]{4,3,2,1,0:T(8,128)}) custom-call(f32[64,128,128]{2,1,0:T(8,128)} %get-tuple-element.21.send_ref), custom_call_target="tpu_custom_call" | custom-call | tf_op jit(solution)/shard_map/exchange/pallas_call | solution.py:253
  130.9 12.9 %all-to-all-start = ((f32[128,48,128]{2,1,0:T(8,128)}), f32[128,48,128]{2,1,0:T(8,128)S(1)}, u32[]{:S(2)}, u32[]{:S(2)}) async-start(f32[128,48,128]{2,1,0:T(8,128)} %get-tuple-element.32), calls=%async_computation | async-start | bytes 6291456 | tf_op jit(solution)/shard_map/all_to_all | solution.py:674
  143.8 4.4 %pivots.1 = (f32[1024,1024]{1,0:T(8,128)}, f32[1024,1024]{1,0:T(8,128)}) custom-call(s32[2,48]{1,0:T(2,128)} %get-tuple-element.19.table_ref, f32[128,128]{1,0:T(8,128)} %bitcast.18, f32[128,80,128]{2,1,0:T(8,128)} %get-tuple-element.25.recv_ref._, f32[128,48,128]{2,1,0:T(8,128)} %get-tuple-element.26.left_ref, f32[16,8,128,128]{3,2,1,0:T(8,128)} %bitcast.5), custom_call_target="tpu_custom_call" | custom-call | tf_op jit(solution)/shard_map/pivots/pallas_call | solution.py:406
  148.2 82.6 %spread.1 = (f32[1024,1024]{1,0:T(8,128)}, f32[128,80,128]{2,1,0:T(8,128)}) custom-call(f32[1024,1024]{1,0:T(8,128)} %get-tuple-element.29.y_ref.own_ref, f32[64,128,128]{2,1,0:T(8,128)} %get-tuple-element.21.send_ref, f32[128,80,128]{2,1,0:T(8,128)} %get-tuple-element.25.recv_ref._), custom_call_target="tpu_custom_call", output_to_operand_aliasing={{1}: (2, {})} | custom-call | tf_op jit(solution)/shard_map/spread/pallas_call | solution.py:538
  230.8 0.0 all-to-all-done
  230.8 0.0 copy-start
  230.8 1.6 copy-done
  232.4 32.3 %update.1 = f32[1024,2048]{1,0:T(8,128)} custom-call(s32[2,48]{1,0:T(2,128)} %get-tuple-element.19.table_ref, f32[128,128]{1,0:T(8,128)} %bitcast.19, f32[1024,1024]{1,0:T(8,128)} %get-tuple-element.28.f_ref, f32[1024,1024]{1,0:T(8,128)} %get-tuple-element.29.y_ref.own_ref, f32[1024,1024]{1,0:T(8,128)} %get-tuple-element.30.came_ref, ...), custom_call_target="tpu_custom_call" | custom-call | tf_op jit(solution)/shard_map/update/pallas_call | solution.py:634
Async XLA Ops:
  130.9 99.8 %all-to-all-start = ((f32[128,48,128]{2,1,0:T(8,128)}), f32[128,48,128]{2,1,0:T(8,128)S(1)}, u32[]{:S(2)}, u32[]{:S(2)}) async-start(f32[128,48,128]{2,1,0:T(8,128)} %get-tuple-element.32), calls=%async_computation | async-start | bytes 6291456 | tf_op jit(solution)/shard_map/all_to_all | solution.py:674
  230.8 1.7 copy-start

commit v4 on v3

--- a/solution.py
+++ b/solution.py
@@ -90,6 +90,62 @@
     )(block_map, child)
 
 
+class Gather:
+    def __init__(self, strip_ref, send_sems, recv_sems, first):
+        self.strip_ref, self.send_sems, self.recv_sems, self.first = strip_ref, send_sems, recv_sems, first
+        self.row, self.col = lax.axis_index("row"), lax.axis_index("col")
+        x, y = self.row % 4, self.row // 4
+        xl, xr, xo = (x + 3) % 4, (x + 1) % 4, (x + 2) % 4
+        yl, yr, yo = (y + 3) % 4, (y + 1) % 4, (y + 2) % 4
+        to = {"xr": y * 4 + xr, "xl": y * 4 + xl, "yr": yr * 4 + x, "yl": yl * 4 + x}
+        lo, hi = pl.ds(0, 4), pl.ds(4, 4)
+        two = [pl.ds(2 * i, 2) for i in range(4)]
+        every, left, right = pl.ds(0, 4), pl.ds(0, 2), pl.ds(2, 2)
+        self.steps = [
+            ((y, x, lo), to["xr"], (y, xl, lo)),
+            ((y, x, lo), to["xl"], (y, xr, lo)),
+            ((y, x, hi), to["yr"], (yl, x, hi)),
+            ((y, x, hi), to["yl"], (yr, x, hi)),
+            ((y, xl, two[0]), to["xr"], (y, xo, two[0])),
+            ((y, xr, two[1]), to["xl"], (y, xo, two[1])),
+            ((yl, x, two[2]), to["yr"], (yo, x, two[2])),
+            ((yr, x, two[3]), to["yl"], (yo, x, two[3])),
+            ((y, every, lo), to["yr"], (yl, every, lo)),
+            ((y, every, lo), to["yl"], (yr, every, lo)),
+            ((every, x, hi), to["xr"], (every, xl, hi)),
+            ((every, x, hi), to["xl"], (every, xr, hi)),
+            ((yl, left, lo), to["yr"], (yo, left, lo)),
+            ((yr, right, lo), to["yl"], (yo, right, lo)),
+            ((left, xl, hi), to["xr"], (left, xo, hi)),
+            ((right, xr, hi), to["xl"], (right, xo, hi)),
+        ]
+
+    def copy(self, step, piece, to_row):
+        ref = self.strip_ref.at[piece]
+        at = step - self.first
+        return pltpu.make_async_remote_copy(
+            ref, ref, self.send_sems.at[at], self.recv_sems.at[at],
+            device_id=(to_row, self.col), device_id_type=MESH,
+        )
+
+    def go(self, *steps):
+        for step in steps:
+            self.copy(step, *self.steps[step][:2]).start()
+
+    def landed(self, *steps):
+        for step in steps:
+            self.copy(step, self.steps[step][2], self.row).wait_recv()
+
+    def left(self, *steps):
+        for step in steps:
+            self.copy(step, *self.steps[step][:2]).wait_send()
+
+    def pass_on(self, first):
+        for step in range(first, first + 4):
+            self.landed(step)
+            self.go(step + 4)
+
+
 def exchange_kernel(
     send_ref, recv_ref, left_ref, strip_ref,
     main_s, main_r, left_s, left_r, col_s, col_r, own_sem, gat_s, gat_r,
@@ -97,19 +153,11 @@
     row, col = lax.axis_index("row"), lax.axis_index("col")
     me = row * 8 + col
     x, y = row % 4, row // 4
-
     top, bottom = pl.ds(0, TOP), pl.ds(TOP, BOT)
-    own = send_ref.at[(row // 2) * 8]
+    own = send_ref.at[(row // 2) * 8 + col]
     own_a = pltpu.make_async_copy(own.at[top], recv_ref.at[me], own_sem.at[0])
+    own_b = pltpu.make_async_copy(send_ref.at[col], strip_ref.at[y, x, col], own_sem.at[1])
     own_c = pltpu.make_async_copy(own.at[bottom], left_ref.at[me], own_sem.at[2])
-    own_b = pltpu.make_async_copy(send_ref.at[col], strip_ref.at[y, x, col], own_sem.at[1])
-
-    @pl.when(col == 0)
-    def _():
-        own_a.start()
-        own_c.start()
-
-    own_b.start()
 
     def send_strip(step, carry):
         to = (col + step) % 8
@@ -119,19 +167,14 @@
         ).start()
         return carry
 
-    lax.fori_loop(1, 8, send_strip, 0)
-
     def send_block(step, carry):
         to = (me + step * 45) % 128
         to_row, to_col = to // 8, to % 8
         block = send_ref.at[(to_row // 2) * 8 + to_col]
-
-        @pl.when((to_col == 0) | (to_col // 2 != col // 2))
-        def _():
-            pltpu.make_async_remote_copy(
-                block.at[top], recv_ref.at[me], main_s, main_r,
-                device_id=(to_row, to_col), device_id_type=MESH,
-            ).start()
+        pltpu.make_async_remote_copy(
+            block.at[top], recv_ref.at[me], main_s, main_r,
+            device_id=(to_row, to_col), device_id_type=MESH,
+        ).start()
 
         @pl.when(to_col == 0)
         def _():
@@ -142,82 +185,39 @@
 
         return carry
 
-    xp, xm = y * 4 + (x + 1) % 4, y * 4 + (x + 3) % 4
-    yp, ym = ((y + 1) % 4) * 4 + x, ((y + 3) % 4) * 4 + x
-    xl, xr = (x + 3) % 4, (x + 1) % 4
-    yl, yr = (y + 3) % 4, (y + 1) % 4
-
-    def hop(index, piece, to_row):
-        ref = strip_ref.at[piece]
-        return pltpu.make_async_remote_copy(
-            ref, ref, gat_s.at[index], gat_r.at[index],
-            device_id=(to_row, col), device_id_type=MESH,
-        )
-
-    def landed(index, piece):
-        ref = strip_ref.at[piece]
-        pltpu.make_async_remote_copy(
-            ref, ref, gat_s.at[index], gat_r.at[index],
-            device_id=(row, col), device_id_type=MESH,
-        ).wait_recv()
-
-    lo, hi = pl.ds(0, 4), pl.ds(4, 4)
-    two = [pl.ds(2 * i, 2) for i in range(4)]
-    every = pl.ds(0, 4)
-
+    own_b.start()
+    lax.fori_loop(1, 8, send_strip, 0)
+    own_a.start()
+
+    @pl.when(col == 0)
+    def _():
+        own_c.start()
+
+    gather = Gather(strip_ref, gat_s, gat_r, 0)
+    lax.fori_loop(1, 17, send_block, 0)
     seven = strip_ref.at[y, x, pl.ds(0, 7)]
     pltpu.make_async_remote_copy(
         seven, seven, col_s, col_r, device_id=(row, col), device_id_type=MESH
     ).wait()
     own_b.wait()
-
-    hops = []
-
-    def go(index, piece, to_row):
-        copy = hop(index, piece, to_row)
-        copy.start()
-        hops.append(copy)
-
-    go(0, (y, x, lo), xp)
-    go(1, (y, x, lo), xm)
-    go(2, (y, x, hi), yp)
-    go(3, (y, x, hi), ym)
-    lax.fori_loop(1, 32, send_block, 0)
-    landed(0, (y, xl, lo))
-    go(4, (y, xl, two[0]), xp)
-    landed(1, (y, xr, lo))
-    go(5, (y, xr, two[1]), xm)
-    landed(2, (yl, x, hi))
-    go(6, (yl, x, two[2]), yp)
-    landed(3, (yr, x, hi))
-    go(7, (yr, x, two[3]), ym)
-    lax.fori_loop(32, 64, send_block, 0)
-    xo, yo = (x + 2) % 4, (y + 2) % 4
-    landed(4, (y, xo, two[0]))
-    landed(5, (y, xo, two[1]))
-    go(8, (y, every, lo), yp)
-    go(9, (y, every, lo), ym)
-    landed(6, (yo, x, two[2]))
-    landed(7, (yo, x, two[3]))
-    go(10, (every, x, hi), xp)
-    go(11, (every, x, hi), xm)
-    lax.fori_loop(64, 96, send_block, 0)
-    first, last = pl.ds(0, 2), pl.ds(2, 2)
-    landed(8, (yl, every, lo))
-    go(12, (yl, first, lo), yp)
-    landed(9, (yr, every, lo))
-    go(13, (yr, last, lo), ym)
-    landed(10, (every, xl, hi))
-    go(14, (first, xl, hi), xp)
-    landed(11, (every, xr, hi))
-    go(15, (last, xr, hi), xm)
-    lax.fori_loop(96, 128, send_block, 0)
-    landed(12, (yo, first, lo))
-    landed(13, (yo, last, lo))
-    landed(14, (first, xo, hi))
-    landed(15, (last, xo, hi))
-    for copy in hops:
-        copy.wait_send()
+    gather.go(0, 1, 2, 3)
+    lax.fori_loop(17, 49, send_block, 0)
+    gather.pass_on(0)
+    lax.fori_loop(49, 81, send_block, 0)
+    gather.landed(4, 5, 6, 7)
+
+    @pl.when(col == 0)
+    def _():
+        gather.go(8, 9, 10, 11)
+
+    lax.fori_loop(81, 105, send_block, 0)
+
+    @pl.when(col == 0)
+    def _():
+        gather.pass_on(8)
+
+    lax.fori_loop(105, 128, send_block, 0)
+    gather.left(*range(8))
 
     def blocks(ref, count, send_sem, recv_sem):
         part = ref.at[pl.ds(0, count)]
@@ -227,25 +227,18 @@
 
     @pl.when(col == 0)
     def _():
-        own_a.wait()
+        gather.landed(12, 13, 14, 15)
+        gather.left(*range(8, 16))
         own_c.wait()
-        blocks(recv_ref, 111, main_s, main_r).wait_send()
         blocks(left_ref, 15, left_s, left_r).wait_send()
-        blocks(recv_ref, 127, main_s, main_r).wait_recv()
         blocks(left_ref, 127, left_s, left_r).wait_recv()
 
-    @pl.when(col == 1)
-    def _():
-        blocks(recv_ref, 112, main_s, main_r).wait_send()
-
-    @pl.when(col > 1)
-    def _():
-        blocks(recv_ref, 96, main_s, main_r).wait_send()
-
     @pl.when(col > 0)
     def _():
         blocks(left_ref, 16, left_s, left_r).wait_send()
-        blocks(recv_ref, 96, main_s, main_r).wait_recv()
+
+    own_a.wait()
+    blocks(recv_ref, 127, main_s, main_r).wait()
 
 
 def exchange(send):
@@ -422,13 +415,14 @@
 
 
 CHUNKS = 16
+WINDOW = 4
+PASS = 10
 
 
 def spread_kernel(
-    y_ref, send_ref, _, out_ref, recv_ref, ring_s, ring_r, core_s, core_r, flat_s, flat_r, own_sem
+    y_ref, _, out_ref, strip_ref, ring_s, ring_r, core_s, core_r, gat_s, gat_r
 ):
     row, col = lax.axis_index("row"), lax.axis_index("col")
-    me = row * 8 + col
     z, core = col // 2, col % 2
     size = TR // CHUNKS
 
@@ -447,43 +441,21 @@
             device_id=(row, z * 2 + 1), device_id_type=MESH,
         )
 
-    def flat(step, carry):
-        to = (row * 2 + core + step * 11) % 32
-        to_row, to_col = to // 2, z * 2 + to % 2
-
-        @pl.when(to_col != 0)
-        def _():
-            pltpu.make_async_remote_copy(
-                send_ref.at[(to_row // 2) * 8 + to_col, pl.ds(0, TOP)], recv_ref.at[me], flat_s, flat_r,
-                device_id=(to_row, to_col), device_id_type=MESH,
-            ).start()
-
-        return carry
-
-    def flats(count):
-        part = recv_ref.at[pl.ds(0, count)]
-        return pltpu.make_async_remote_copy(
-            part, part, flat_s, flat_r, device_id=(row, col), device_id_type=MESH
-        )
-
-    own = pltpu.make_async_copy(
-        send_ref.at[(row // 2) * 8 + col, pl.ds(0, TOP)], recv_ref.at[me], own_sem
-    )
+    gather = Gather(strip_ref, gat_s, gat_r, 8)
 
     @pl.when(col != 0)
     def _():
-        own.start()
+        gather.go(8, 9, 10, 11)
 
     @pl.when(col == 0)
     def _():
         for t in range(CHUNKS):
-            if t >= 4:
-                ring(y_ref, t - 4).wait_send()
+            if t >= WINDOW:
+                ring(y_ref, t - WINDOW).wait_send()
             ring(y_ref, t).start()
             across(y_ref, t).start()
-            lax.fori_loop(max(2 * t, 1), 2 * t + 2, flat, 0)
         for t in range(CHUNKS):
-            if t >= CHUNKS - 4:
+            if t >= CHUNKS - WINDOW:
                 ring(y_ref, t).wait_send()
             across(y_ref, t).wait_send()
 
@@ -497,7 +469,8 @@
             if goes(t):
                 ring(out_ref, t).start()
             across(out_ref, t).start()
-            lax.fori_loop(max(2 * n, 1), 2 * n + 2, flat, 0)
+            if n == PASS:
+                gather.pass_on(8)
         for t in range(CHUNKS):
             if goes(t):
                 ring(out_ref, t).wait_send()
@@ -511,50 +484,38 @@
 
     @pl.when(core == 1)
     def _():
-        lax.fori_loop(1, 32, flat, 0)
+        gather.pass_on(8)
         for t in range(CHUNKS):
             across(out_ref, t).wait_recv()
 
-    @pl.when(col == 0)
-    def _():
-        flats(16).wait_send()
-
-    @pl.when(col == 1)
-    def _():
-        flats(15).wait_send()
-
-    @pl.when(col > 1)
-    def _():
-        flats(31).wait_send()
-
     @pl.when(col != 0)
     def _():
-        flats(31).wait_recv()
-        own.wait()
-
-
-def spread(y, send, recv):
+        gather.landed(12, 13, 14, 15)
+        gather.left(*range(8, 16))
+
+
+def spread(y, strips):
     dma = pltpu.SemaphoreType.DMA
     return pl.pallas_call(
         spread_kernel,
         out_shape=(
             jax.ShapeDtypeStruct((TR, TR), jnp.float32),
-            jax.ShapeDtypeStruct((128, TOP, BLK), jnp.float32),
+            jax.ShapeDtypeStruct((4, 4, 8, BLK, BLK), jnp.float32),
         ),
-        in_specs=[HBM, HBM, HBM],
+        in_specs=[HBM, HBM],
         out_specs=(HBM, HBM),
-        input_output_aliases={2: 1},
+        input_output_aliases={1: 1},
         scratch_shapes=[
-            dma((CHUNKS,)), dma((CHUNKS,)), dma((CHUNKS,)), dma((CHUNKS,)), dma, dma, dma,
+            dma((CHUNKS,)), dma((CHUNKS,)), dma((CHUNKS,)), dma((CHUNKS,)), dma((8,)), dma((8,)),
         ],
         compiler_params=pltpu.CompilerParams(has_side_effects=True, vmem_limit_bytes=VMEM_LIMIT),
         name="spread",
-    )(y, send, recv)
+    )(y, strips)
 
 
 def update_kernel(table_ref, diag_ref, f_ref, own_ref, came_ref, *refs):
     strips, tops, bottoms = refs[0:4], refs[4:8], refs[8:12]
-    out_ref, y, yh, yl, uh, ul, sem = refs[12:]
+    out_ref, y, yc, uc, sem = refs[12:]
     row, col = lax.axis_index("row"), lax.axis_index("col")
     step = pl.program_id(0)
 
@@ -572,7 +533,8 @@
             copy.start()
             copy.wait()
 
-        yh[...], yl[...] = split(y[...])
+        yc[:, :TR], yc[:, 2 * TR :] = split(y[...])
+        yc[:, TR : 2 * TR] = yc[:, :TR]
 
     factors = (col == 0) & (step < 4)
 
@@ -585,24 +547,25 @@
         for u in range(2):
             j = step * 2 + u
 
-            def strip_block(i, carry):
+            def strip_block(i):
                 on = identity(BLK) & (col * 16 + j == i)
                 total = jnp.where(on, diag_ref[pl.ds(i, 1), :], 0.0)
                 for k in range(2):
                     g, h = table_ref[k, 24 + i], table_ref[k, 8 + j]
                     value = strips[2 * u + k][0, jnp.maximum(g, 0), 0]
                     total = total + jnp.where((g >= 0) & (h >= 0), value, 0.0)
-                at = pl.ds(pl.multiple_of(i * BLK, BLK), BLK)
-                uh[at, pl.ds(u * BLK, BLK)], ul[at, pl.ds(u * BLK, BLK)] = split(total)
-                return carry
-
-            lax.fori_loop(0, 8, strip_block, 0)
-
-        out_ref[...] = dot3((yh[...], yl[...]), (uh[...], ul[...]))
+                high, low = split(total)
+                for part, value in enumerate((high, low, high)):
+                    uc[pl.ds(part * TR + i * BLK, BLK), pl.ds(u * BLK, BLK)] = value
+
+            for i in range(8):
+                strip_block(i)
+
+        out_ref[...] = dot1(yc[...], uc[...])
         for u in range(2):
             j = step * 2 + u
 
-            def front_block(i, carry):
+            def front_block(i):
                 for refs, first, count in ((tops, 0, TOP), (bottoms, TOP, BOT)):
                     there = lax.broadcasted_iota(jnp.int32, (count, BLK), 0) + first
                     on = (there == lax.broadcasted_iota(jnp.int32, (count, BLK), 1)) & (
@@ -613,11 +576,11 @@
                         g, h = table_ref[k, i], table_ref[k, 8 + j]
                         value = refs[2 * u + k][0, jnp.maximum(g, 0), 0]
                         total = total + jnp.where((g >= 0) & (h >= 0), value, 0.0)
-                    at = pl.ds(pl.multiple_of(i * BLK + first, 16), count), pl.ds(u * BLK, BLK)
+                    at = pl.ds(i * BLK + first, count), pl.ds(u * BLK, BLK)
                     out_ref[at] = total - out_ref[at]
-                return carry
-
-            lax.fori_loop(0, 8, front_block, 0)
+
+            for i in range(8):
+                front_block(i)
 
 
 def update(table, diag, factors, own, came, strips, recv, rest):
@@ -649,10 +612,8 @@
             out_specs=pl.BlockSpec((TR, 256), lambda s, table: (0, s)),
             scratch_shapes=[
                 pltpu.VMEM((TR, TR), f32),
-                pltpu.VMEM((TR, TR), bf16),
-                pltpu.VMEM((TR, TR), bf16),
-                pltpu.VMEM((TR, 256), bf16),
-                pltpu.VMEM((TR, 256), bf16),
+                pltpu.VMEM((TR, 3 * TR), bf16),
+                pltpu.VMEM((3 * TR, 256), bf16),
                 pltpu.SemaphoreType.DMA,
             ],
         ),
@@ -672,9 +633,8 @@
     recv, left, strips = exchange(send)
     rest, recv, left, strips = lax.optimization_barrier((rest, recv, left, strips))
     rest = lax.all_to_all(rest, ("row", "col"), split_axis=0, concat_axis=0, tiled=True)
-    strips = strips.reshape(16, 8, BLK, BLK)
-    y, factors = pivots(table, diag, recv, left, strips)
-    came, recv = spread(y, send, recv)
+    y, factors = pivots(table, diag, recv, left, strips.reshape(16, 8, BLK, BLK))
+    came, strips = spread(y, strips)
     return update(table, diag, factors, y, came, strips, recv, rest)
 
 

time: 267 us -> 248 us (0.929)
  Pallas kernels: 250 us -> 235 us
  starting transfers between devices: 12.9 us -> 9.58 us
    pallas_call x1, Pallas kernels: 122 us -> 111 us  [exchange(): pl.pallas_call(exchange_kernel, out_shape=(jax.ShapeDtypeStruct((128, TOP...]
    pallas_call x1, Pallas kernels: 32.3 us -> 27.7 us  [update(): pl.pallas_call(update_kernel, out_shape=jax.ShapeDtypeStruct((TR, TC), f3...]
    all_to_all x1, starting transfers between devices: 12.9 us -> 9.58 us  [body(): lax.all_to_all(rest, ('row', 'col'), split_axis=0, concat_axis=0, tiled=T...]
  transfers between devices with their start and end apart: 1 -> 1, of which waited for: 0 -> 0; matrix products, arithmetic and copies ran while one was open for 0% -> 0% of each run, Pallas kernels for 33% -> 35%
where the time goes in v4:
time: 248 us; the launch traced here: 247 us
  Pallas kernels  235 us (95%)
  starting transfers between devices  9.58 us (4%)
    pallas_call x1, Pallas kernels, exchange(): pl.pallas_call(exchange_kernel, out_shape=(jax.ShapeDtypeStruct((128, TOP...  111 us
    pallas_call x1, Pallas kernels, spread(): pl.pallas_call(spread_kernel, out_shape=(jax.ShapeDtypeStruct((TR, TR), j...  83.1 us
    pallas_call x1, Pallas kernels, update(): pl.pallas_call(update_kernel, out_shape=jax.ShapeDtypeStruct((TR, TC), f3...  27.7 us
    all_to_all x1, starting transfers between devices, body(): lax.all_to_all(rest, ('row', 'col'), split_axis=0, concat_axis=0, tiled=T...  9.58 us
    pallas_call x1, Pallas kernels, pack(): pl.pallas_call(pack_kernel, out_shape=(jax.ShapeDtypeStruct((64, BLK, BLK...  9.3 us
  transfers between devices with their start and end apart: 1, of which 0 were waited for; matrix products, arithmetic and copies ran while one was open for 0% of the time, Pallas kernels for 35%

profile of v4, /device:TPU:33, one launch (start us, length us, event | category | flops | bytes accessed | tf_op | source)
XLA Modules:
  0.0 246.6 jit_solution(14915556155087567355)
XLA Ops:
  0.0 9.3 %pack.1 = (f32[64,128,128]{2,1,0:T(8,128)}, f32[128,48,128]{2,1,0:T(8,128)}, s32[2,48]{1,0:T(2,128)}) custom-call(s32[2,64]{1,0:T(2,128)} %map_ref.1, f32[1024,1024]{1,0:T(8,128)} %child_ref.1), custom_call_target="tpu_custom_call" | custom-call | tf_op jit(solution)/shard_map/pack/pallas_call | solution.py:78
  9.3 110.8 %exchange.1 = (f32[128,80,128]{2,1,0:T(8,128)}, f32[128,48,128]{2,1,0:T(8,128)}, f32[4,4,8,128,128]{4,3,2,1,0:T(8,128)}) custom-call(f32[64,128,128]{2,1,0:T(8,128)} %get-tuple-element.21.send_ref), custom_call_target="tpu_custom_call" | custom-call | tf_op jit(solution)/shard_map/exchange/pallas_call | solution.py:246
  120.1 9.6 %all-to-all-start = ((f32[128,48,128]{2,1,0:T(8,128)}), f32[128,48,128]{2,1,0:T(8,128)S(1)}, u32[]{:S(2)}, u32[]{:S(2)}) async-start(f32[128,48,128]{2,1,0:T(8,128)} %get-tuple-element.32), calls=%async_computation | async-start | bytes 6291456 | tf_op jit(solution)/shard_map/all_to_all | solution.py:635
  129.7 4.4 %pivots.1 = (f32[1024,1024]{1,0:T(8,128)}, f32[1024,1024]{1,0:T(8,128)}) custom-call(s32[2,48]{1,0:T(2,128)} %get-tuple-element.19.table_ref, f32[128,128]{1,0:T(8,128)} %bitcast.18, f32[128,80,128]{2,1,0:T(8,128)} %get-tuple-element.25.recv_ref, f32[128,48,128]{2,1,0:T(8,128)} %get-tuple-element.26.left_ref, f32[16,8,128,128]{3,2,1,0:T(8,128)} %bitcast.5), custom_call_target="tpu_custom_call" | custom-call | tf_op jit(solution)/shard_map/pivots/pallas_call | solution.py:399
  134.0 83.1 %spread.1 = (f32[1024,1024]{1,0:T(8,128)}, f32[4,4,8,128,128]{4,3,2,1,0:T(8,128)}) custom-call(f32[1024,1024]{1,0:T(8,128)} %get-tuple-element.29.y_ref.own_ref, f32[4,4,8,128,128]{4,3,2,1,0:T(8,128)} %get-tuple-element.27._), custom_call_target="tpu_custom_call", output_to_operand_aliasing={{1}: (1, {})} | custom-call | tf_op jit(solution)/shard_map/spread/pallas_call | solution.py:499
  217.1 0.0 all-to-all-done
  217.1 0.0 copy-start
  217.1 1.6 copy-done
  218.8 27.7 %update.1 = f32[1024,2048]{1,0:T(8,128)} custom-call(s32[2,48]{1,0:T(2,128)} %get-tuple-element.19.table_ref, f32[128,128]{1,0:T(8,128)} %bitcast.19, f32[1024,1024]{1,0:T(8,128)} %get-tuple-element.28.f_ref, f32[1024,1024]{1,0:T(8,128)} %get-tuple-element.29.y_ref.own_ref, f32[1024,1024]{1,0:T(8,128)} %get-tuple-element.30.came_ref, ...), custom_call_target="tpu_custom_call" | custom-call | tf_op jit(solution)/shard_map/update/pallas_call | solution.py:597
Async XLA Ops:
  120.1 97.0 %all-to-all-start = ((f32[128,48,128]{2,1,0:T(8,128)}), f32[128,48,128]{2,1,0:T(8,128)S(1)}, u32[]{:S(2)}, u32[]{:S(2)}) async-start(f32[128,48,128]{2,1,0:T(8,128)} %get-tuple-element.32), calls=%async_computation | async-start | bytes 6291456 | tf_op jit(solution)/shard_map/all_to_all | solution.py:635
  217.1 1.7 copy-start

commit v5 on v4

--- a/solution.py
+++ b/solution.py
@@ -7,7 +7,7 @@
 
 BLK = 128
 PW = 512
-TOP = 80
+TOP = 64
 BOT = BLK - TOP
 TR = 1024
 TC = 2048
@@ -168,8 +168,9 @@
         return carry
 
     def send_block(step, carry):
-        to = (me + step * 45) % 128
-        to_row, to_col = to // 8, to % 8
+        way = (step * 37) % 128
+        to_row = ((y + way // 4) % 4) * 4 + (x + way) % 4
+        to_col = ((col // 2 + way // 16) % 4) * 2 + (col + way // 64) % 2
         block = send_ref.at[(to_row // 2) * 8 + to_col]
         pltpu.make_async_remote_copy(
             block.at[top], recv_ref.at[me], main_s, main_r,

time: 248 us -> 234 us (0.944)
  Pallas kernels: 235 us -> 225 us
    pallas_call x1, Pallas kernels: 111 us -> 101 us  [exchange(): pl.pallas_call(exchange_kernel, out_shape=(jax.ShapeDtypeStruct((128, TOP...]
  transfers between devices with their start and end apart: 1 -> 1, of which waited for: 0 -> 0; matrix products, arithmetic and copies ran while one was open for 0% -> 0% of each run, Pallas kernels for 35% -> 37%
where the time goes in v5:
time: 234 us; the launch traced here: 233 us
  Pallas kernels  225 us (96%)
  starting transfers between devices  8.14 us (3%)
    pallas_call x1, Pallas kernels, exchange(): pl.pallas_call(exchange_kernel, out_shape=(jax.ShapeDtypeStruct((128, TOP...  101 us
    pallas_call x1, Pallas kernels, spread(): pl.pallas_call(spread_kernel, out_shape=(jax.ShapeDtypeStruct((TR, TR), j...  82.3 us
    pallas_call x1, Pallas kernels, update(): pl.pallas_call(update_kernel, out_shape=jax.ShapeDtypeStruct((TR, TC), f3...  27.7 us
    pallas_call x1, Pallas kernels, pack(): pl.pallas_call(pack_kernel, out_shape=(jax.ShapeDtypeStruct((64, BLK, BLK...  9.47 us
    all_to_all x1, starting transfers between devices, body(): lax.all_to_all(rest, ('row', 'col'), split_axis=0, concat_axis=0, tiled=T...  8.14 us
  transfers between devices with their start and end apart: 1, of which 0 were waited for; matrix products, arithmetic and copies ran while one was open for 0% of the time, Pallas kernels for 37%

profile of v5, /device:TPU:33, one launch (start us, length us, event | category | flops | bytes accessed | tf_op | source)
XLA Modules:
  0.0 233.3 jit_solution(6203301642073959975)
XLA Ops:
  0.0 9.5 %pack.1 = (f32[64,128,128]{2,1,0:T(8,128)}, f32[128,64,128]{2,1,0:T(8,128)}, s32[2,48]{1,0:T(2,128)}) custom-call(s32[2,64]{1,0:T(2,128)} %map_ref.1, f32[1024,1024]{1,0:T(8,128)} %child_ref.1), custom_call_target="tpu_custom_call" | custom-call | tf_op jit(solution)/shard_map/pack/pallas_call | solution.py:78
  9.5 101.1 %exchange.1 = (f32[128,64,128]{2,1,0:T(8,128)}, f32[128,64,128]{2,1,0:T(8,128)}, f32[4,4,8,128,128]{4,3,2,1,0:T(8,128)}) custom-call(f32[64,128,128]{2,1,0:T(8,128)} %get-tuple-element.21.send_ref), custom_call_target="tpu_custom_call" | custom-call | tf_op jit(solution)/shard_map/exchange/pallas_call | solution.py:247
  110.6 8.1 %all-to-all-start = ((f32[128,64,128]{2,1,0:T(8,128)}), f32[128,64,128]{2,1,0:T(8,128)}, u32[]{:S(2)}, u32[]{:S(2)}) async-start(f32[128,64,128]{2,1,0:T(8,128)} %get-tuple-element.32), calls=%async_computation | async-start | bytes 8388608 | tf_op jit(solution)/shard_map/all_to_all | solution.py:636
  118.7 4.4 %pivots.1 = (f32[1024,1024]{1,0:T(8,128)}, f32[1024,1024]{1,0:T(8,128)}) custom-call(s32[2,48]{1,0:T(2,128)} %get-tuple-element.19.table_ref, f32[128,128]{1,0:T(8,128)} %bitcast.14, f32[128,64,128]{2,1,0:T(8,128)} %get-tuple-element.25.recv_ref, f32[128,64,128]{2,1,0:T(8,128)} %get-tuple-element.26.left_ref, f32[16,8,128,128]{3,2,1,0:T(8,128)} %bitcast.5), custom_call_target="tpu_custom_call" | custom-call | tf_op jit(solution)/shard_map/pivots/pallas_call | solution.py:400
  123.1 82.3 %spread.1 = (f32[1024,1024]{1,0:T(8,128)}, f32[4,4,8,128,128]{4,3,2,1,0:T(8,128)}) custom-call(f32[1024,1024]{1,0:T(8,128)} %get-tuple-element.29.y_ref.own_ref, f32[4,4,8,128,128]{4,3,2,1,0:T(8,128)} %get-tuple-element.27._), custom_call_target="tpu_custom_call", output_to_operand_aliasing={{1}: (1, {})} | custom-call | tf_op jit(solution)/shard_map/spread/pallas_call | solution.py:500
  205.4 0.0 all-to-all-done
  205.4 27.7 %update.1 = f32[1024,2048]{1,0:T(8,128)} custom-call(s32[2,48]{1,0:T(2,128)} %get-tuple-element.19.table_ref, f32[128,128]{1,0:T(8,128)} %bitcast.15, f32[1024,1024]{1,0:T(8,128)} %get-tuple-element.28.f_ref, f32[1024,1024]{1,0:T(8,128)} %get-tuple-element.29.y_ref.own_ref, f32[1024,1024]{1,0:T(8,128)} %get-tuple-element.30.came_ref, ...), custom_call_target="tpu_custom_call" | custom-call | tf_op jit(solution)/shard_map/update/pallas_call | solution.py:598
Async XLA Ops:
  110.6 94.9 %all-to-all-start = ((f32[128,64,128]{2,1,0:T(8,128)}), f32[128,64,128]{2,1,0:T(8,128)}, u32[]{:S(2)}, u32[]{:S(2)}) async-start(f32[128,64,128]{2,1,0:T(8,128)} %get-tuple-element.32), calls=%async_computation | async-start | bytes 8388608 | tf_op jit(solution)/shard_map/all_to_all | solution.py:636

commit v6 on v5

--- a/solution.py
+++ b/solution.py
@@ -24,9 +24,9 @@
     child, group = row // 8, row % 8
 
     def start(step, carry):
-        t, u = step // 8, step % 8
-        q = map_ref[child, group * 8 + t] // 16
-        c = map_ref[child, col * 8 + u] // 16
+        t, u = step >> 3, step & 7
+        q = map_ref[child, group * 8 + t] >> 4
+        c = map_ref[child, col * 8 + u] >> 4
         block = child_ref.at[
             pl.ds(pl.multiple_of(t * BLK, BLK), BLK), pl.ds(pl.multiple_of(u * BLK, BLK), BLK)
         ]
@@ -38,33 +38,33 @@
         pltpu.make_async_copy(rest, rest_ref.at[q * 16 + 8 + c], rest_sem).start()
         return carry
 
-    lax.fori_loop(0, 64, start, 0)
+    lax.fori_loop(0, 64, start, 0, unroll=8)
 
     def clear(step, carry):
         table_ref[step // 32, step % 32] = -1
         return carry
 
-    lax.fori_loop(0, 64, clear, 0)
+    lax.fori_loop(0, 64, clear, 0, unroll=8)
 
     def look(step, carry):
-        k, s = step // 64, step % 64
+        k, s = step >> 6, step & 63
         b = map_ref[k, s]
 
-        @pl.when(b // 8 == row)
-        def _():
-            table_ref[k, b % 8] = s // 8
-
-        @pl.when(b // 16 == col)
-        def _():
-            table_ref[k, 8 + b % 16] = s // 8
+        @pl.when(b >> 3 == row)
+        def _():
+            table_ref[k, b & 7] = s >> 3
+
+        @pl.when(b >> 4 == col)
+        def _():
+            table_ref[k, 8 + (b & 15)] = s >> 3
 
         @pl.when(b < 8)
         def _():
-            table_ref[k, 24 + b] = s // 8
+            table_ref[k, 24 + b] = s >> 3
 
         return carry
 
-    lax.fori_loop(0, 128, look, 0)
+    lax.fori_loop(0, 128, look, 0, unroll=8)
     for k in range(2):
         for j in range(16):
             here = table_ref[k, 8 + j]

time: 234 us -> 231 us (0.987)
  Pallas kernels: 225 us -> 222 us
    pallas_call x1, Pallas kernels: 9.47 us -> 5.99 us  [pack(): pl.pallas_call(pack_kernel, out_shape=(jax.ShapeDtypeStruct((64, BLK, BLK...]
  transfers between devices with their start and end apart: 1 -> 1, of which waited for: 0 -> 0; matrix products, arithmetic and copies ran while one was open for 0% -> 0% of each run, Pallas kernels for 37% -> 38%
where the time goes in v6:
time: 231 us; the launch traced here: 230 us
  Pallas kernels  222 us (96%)
  starting transfers between devices  8.14 us (4%)
    pallas_call x1, Pallas kernels, exchange(): pl.pallas_call(exchange_kernel, out_shape=(jax.ShapeDtypeStruct((128, TOP...  101 us
    pallas_call x1, Pallas kernels, spread(): pl.pallas_call(spread_kernel, out_shape=(jax.ShapeDtypeStruct((TR, TR), j...  82.5 us
    pallas_call x1, Pallas kernels, update(): pl.pallas_call(update_kernel, out_shape=jax.ShapeDtypeStruct((TR, TC), f3...  27.9 us
    all_to_all x1, starting transfers between devices, body(): lax.all_to_all(rest, ('row', 'col'), split_axis=0, concat_axis=0, tiled=T...  8.14 us
    pallas_call x1, Pallas kernels, pack(): pl.pallas_call(pack_kernel, out_shape=(jax.ShapeDtypeStruct((64, BLK, BLK...  5.99 us
  transfers between devices with their start and end apart: 1, of which 0 were waited for; matrix products, arithmetic and copies ran while one was open for 0% of the time, Pallas kernels for 38%

profile of v6, /device:TPU:33, one launch (start us, length us, event | category | flops | bytes accessed | tf_op | source)
XLA Modules:
  0.0 230.2 jit_solution(9952232708526220990)
XLA Ops:
  0.0 6.0 %pack.1 = (f32[64,128,128]{2,1,0:T(8,128)}, f32[128,64,128]{2,1,0:T(8,128)}, s32[2,48]{1,0:T(2,128)}) custom-call(s32[2,64]{1,0:T(2,128)} %map_ref.1, f32[1024,1024]{1,0:T(8,128)} %child_ref.1), custom_call_target="tpu_custom_call" | custom-call | tf_op jit(solution)/shard_map/pack/pallas_call | solution.py:78
  6.0 101.1 %exchange.1 = (f32[128,64,128]{2,1,0:T(8,128)}, f32[128,64,128]{2,1,0:T(8,128)}, f32[4,4,8,128,128]{4,3,2,1,0:T(8,128)}) custom-call(f32[64,128,128]{2,1,0:T(8,128)} %get-tuple-element.21.send_ref), custom_call_target="tpu_custom_call" | custom-call | tf_op jit(solution)/shard_map/exchange/pallas_call | solution.py:247
  107.1 8.1 %all-to-all-start = ((f32[128,64,128]{2,1,0:T(8,128)}), f32[128,64,128]{2,1,0:T(8,128)}, u32[]{:S(2)}, u32[]{:S(2)}) async-start(f32[128,64,128]{2,1,0:T(8,128)} %get-tuple-element.32), calls=%async_computation | async-start | bytes 8388608 | tf_op jit(solution)/shard_map/all_to_all | solution.py:636
  115.2 4.4 %pivots.1 = (f32[1024,1024]{1,0:T(8,128)}, f32[1024,1024]{1,0:T(8,128)}) custom-call(s32[2,48]{1,0:T(2,128)} %get-tuple-element.19.table_ref, f32[128,128]{1,0:T(8,128)} %bitcast.14, f32[128,64,128]{2,1,0:T(8,128)} %get-tuple-element.25.recv_ref, f32[128,64,128]{2,1,0:T(8,128)} %get-tuple-element.26.left_ref, f32[16,8,128,128]{3,2,1,0:T(8,128)} %bitcast.5), custom_call_target="tpu_custom_call" | custom-call | tf_op jit(solution)/shard_map/pivots/pallas_call | solution.py:400
  119.6 82.5 %spread.1 = (f32[1024,1024]{1,0:T(8,128)}, f32[4,4,8,128,128]{4,3,2,1,0:T(8,128)}) custom-call(f32[1024,1024]{1,0:T(8,128)} %get-tuple-element.29.y_ref.own_ref, f32[4,4,8,128,128]{4,3,2,1,0:T(8,128)} %get-tuple-element.27._), custom_call_target="tpu_custom_call", output_to_operand_aliasing={{1}: (1, {})} | custom-call | tf_op jit(solution)/shard_map/spread/pallas_call | solution.py:500
  202.1 0.0 all-to-all-done
  202.2 27.9 %update.1 = f32[1024,2048]{1,0:T(8,128)} custom-call(s32[2,48]{1,0:T(2,128)} %get-tuple-element.19.table_ref, f32[128,128]{1,0:T(8,128)} %bitcast.15, f32[1024,1024]{1,0:T(8,128)} %get-tuple-element.28.f_ref, f32[1024,1024]{1,0:T(8,128)} %get-tuple-element.29.y_ref.own_ref, f32[1024,1024]{1,0:T(8,128)} %get-tuple-element.30.came_ref, ...), custom_call_target="tpu_custom_call" | custom-call | tf_op jit(solution)/shard_map/update/pallas_call | solution.py:598
Async XLA Ops:
  107.1 95.1 %all-to-all-start = ((f32[128,64,128]{2,1,0:T(8,128)}), f32[128,64,128]{2,1,0:T(8,128)}, u32[]{:S(2)}, u32[]{:S(2)}) async-start(f32[128,64,128]{2,1,0:T(8,128)} %get-tuple-element.32), calls=%async_computation | async-start | bytes 8388608 | tf_op jit(solution)/shard_map/all_to_all | solution.py:636
